TPU v7x, 32 devices: a whole 2x2x4 slice. The times are simulated.
32 devices in a mesh: sub: 32 (over z, y, x, core).
Axes of the slice: x: 2, y: 2, z: 4, core: 2. Of those that a mesh axis runs over, the one named last changes fastest.
Arguments:
- stiffness: bfloat16 [32, 1536, 1536], P('sub'), may hold values from -2 to 5, as said below
- local_inverse: bfloat16 [32, 1536, 1536], P('sub'), may hold values from -0.2 to 0.5, as said below
- coarse_basis: float32 [32, 48, 1536], P('sub'), may hold values from -0.15625 to 0.15625
- loads: float32 [32, 1536, 128], P('sub'), may hold values from -8 to 8
- counts: int32 [32, 1536], P('sub'), may hold values from 1 to 2, as said below
- shared_rows: int32 [32, 4, 256], P('sub'), may hold values from 0 to 1536, as said below
- coarse_map: int32 [32, 48], P('sub'), may hold values from 0 to 4095
- coarse_inverse: float32 [4096, 4096], P('sub'), may hold values from -1 to 2, as said below
Outputs:
- solution: float32 [32, 1536, 128], P('sub')
- residual: float32 [32, 1536, 128], P('sub')
Inputs may be any that keep to these rules, and one draw needn't show every extreme that they name: `shared_rows`: for k = 0..3 entry [s, k, t] names a row of subdomain s shared with its slot-k neighbour, or 1536 where unused; live entries come first; entry t of s's list for a neighbour and entry t of that neighbour's list for s name the same unknown; no row appears in two lists of one subdomain; some pair of each kind has exactly 256 live entries. `counts`: 1 plus the number of lists of its subdomain that name the row. `stiffness`: Symmetric. `local_inverse`: Symmetric. `coarse_inverse`: Symmetric. `coarse_map`: A subdomain may name a coarse unknown more than once.
All inputs are finite; a program needn't handle non-finite values.
Results may differ from a plain program's by a relative error of at most 0.0081.
Values sent between devices are 32-bit elements; how exact they have to be, the bound alone decides.
No kernel may reach another device: no remote copies, remote signals or barrier semaphores. Data moves between devices by JAX's collectives and lax.ppermute only.
A program may use at most 128 MiB of HBM per device.

v0:
```python
import functools

import jax
import jax.numpy as jnp
from jax import lax
from jax.experimental import pallas as pl
from jax.experimental.pallas import tpu as pltpu
from jax.sharding import PartitionSpec as P

STRIDE = 8
F32 = jnp.float32
BF16 = jnp.bfloat16
TILE = 512
FINE = 256
HALF = 768
SLOTS = 512
SCAL = 8
ORDER = (3, 1, 2, 0)
LANES = 128

VSPEC = pl.BlockSpec(memory_space=pltpu.VMEM)
SSPEC = pl.BlockSpec(memory_space=pltpu.SMEM)
ASPEC = pl.BlockSpec(memory_space=pltpu.HBM)


def near(shape, dtype=F32):
    return pltpu.VMEM(shape, dtype)


def far(shape, dtype=F32):
    return jax.ShapeDtypeStruct(shape, dtype)


def away(shape, dtype=F32):
    return pltpu.HBM(shape, dtype)


def held(*arrays):
    return tuple(pltpu.with_memory_space_constraint(a, pltpu.VMEM) for a in arrays)


def aside(*arrays):
    return tuple(pltpu.with_memory_space_constraint(a, pltpu.HBM) for a in arrays)


def call(kernel, name, args, outs, scratch=(), specs=None, us=2, mib=16, sent=()):
    specs = specs or {}
    return pl.pallas_call(
        kernel,
        name=name,
        out_shape=tuple(outs),
        in_specs=[specs.get(i, VSPEC) for i in range(len(args))],
        out_specs=tuple(ASPEC if i in sent else VSPEC for i in range(len(outs))),
        scratch_shapes=list(scratch),
        compiler_params=pltpu.CompilerParams(vmem_limit_bytes=mib * 1024 * 1024),
        cost_estimate=pl.CostEstimate(
            flops=0, bytes_accessed=us * 3_000_000, transcendentals=0
        ),
    )(*args)


def cut(x):
    high = x.astype(BF16)
    return high, (x - high.astype(F32)).astype(BF16)


def pair(x):
    return jnp.concatenate(cut(x), axis=1)


def halves(product):
    half = product.shape[1] // 2
    return product[:, :half] + product[:, half:]


def three(product, rows):
    half = product.shape[1] // 2
    return product[:rows, :half] + product[:rows, half:] + product[rows : 2 * rows, :half]


def dot(a, b):
    return jnp.dot(a, b, preferred_element_type=F32)


def tiles(total, step=TILE):
    step = min(step, total)
    return [(lo, min(step, total - lo)) for lo in range(0, total, step)]


def folded(x):
    return jnp.sum(x.reshape(-1, 8, x.shape[-1]), axis=0)


def pick_out(pick_ref, cat_ref, out_refs):
    cap = out_refs[0].shape[0]
    for j, out in enumerate(out_refs):
        out[...] = halves(dot(pick_ref[j * cap : (j + 1) * cap, :], cat_ref[...]))


def arrivals(arrived_refs, arr_cat):
    cap = arrived_refs[0].shape[0]
    for j, ref in enumerate(arrived_refs):
        arr_cat[j * cap : (j + 1) * cap, :] = pair(ref[...])


def bring(pairs, sems):
    copies = [pltpu.make_async_copy(*p, sems.at[i]) for i, p in enumerate(pairs)]
    for copy in copies:
        copy.start()
    return copies


def each(total, step, work, flat=False):
    if flat:
        for lo in range(0, total, step):
            work(lo)
        return

    def one(i, carry):
        work(pl.multiple_of(i * step, step))
        return carry

    lax.fori_loop(0, total // step, one, 0)


def summed(total, step, work, start):
    def one(i, carry):
        return work(pl.multiple_of(i * step, step), carry)

    return lax.fori_loop(0, total // step, one, start)


def fill_pick(row_ref, pick_ref):
    slots, rows = pick_ref.shape

    def some(lo):
        listed = row_ref[:, pl.ds(lo, LANES)].astype(F32)
        entries = jnp.broadcast_to(listed, (LANES, LANES)).T
        for left in range(0, rows, LANES):
            at = left + lax.broadcasted_iota(jnp.int32, (LANES, LANES), 1)
            same = jnp.where(at.astype(F32) == entries, 1.0, 0.0)
            pick_ref[pl.ds(lo, LANES), left : left + LANES] = same.astype(BF16)

    each(slots, LANES, some)


def fill_place(row_ref, place_ref):
    rows, slots = place_ref.shape

    def some(lo):
        at = lo + lax.broadcasted_iota(jnp.int32, (LANES, slots), 0)
        same = jnp.where(at == row_ref[...], 1.0, 0.0)
        place_ref[pl.ds(lo, LANES), :] = same.astype(BF16)

    each(rows, LANES, some)


def weights_of(count_ref):
    rows = count_ref.shape[1]
    return jnp.broadcast_to(1.0 / count_ref[...].astype(F32), (LANES, rows)).T


def fill_basis2(basis_ref, basis2_ref):
    ncl = basis_ref.shape[0]
    high, low = cut(basis_ref[...])
    basis2_ref[:ncl, :] = high
    basis2_ref[ncl:, :] = low


def loads_kernel(rows_ref, loads_from, listed_ref, out0, out1, out2, out3, pick, cat, loads, sems):
    copies = bring([(loads_from, loads)], sems)
    me = lax.axis_index("sub")
    one = me % 2 == 0
    far_one = (me // STRIDE) % 2 == 0
    given = [rows_ref[k : k + 1, :] for k in range(4)]
    lists = [
        jnp.where(one, given[0], given[1]),
        jnp.where(one, given[1], given[0]),
        jnp.where(far_one, given[2], given[3]),
        jnp.where(far_one, given[3], given[2]),
    ]
    listed_ref[...] = jnp.concatenate([lists[j] for j in ORDER], axis=1)
    fill_pick(listed_ref, pick)
    for copy in copies:
        copy.wait()
    for lo, n in tiles(loads.shape[0]):
        cat[lo : lo + n, :] = pair(loads[lo : lo + n, :])
    pick_out(pick, cat, (out0, out1, out2, out3))


def fill_basis3(basis_ref, basis3_ref):
    ncl, rows = basis_ref.shape
    high, low = cut(basis_ref[...])
    high, low = high.astype(F32), low.astype(F32)
    fill = jnp.zeros((basis3_ref.shape[1] - 3 * ncl, rows), F32)
    basis3_ref[...] = jnp.concatenate([high, high, low, fill], axis=0).T.astype(BF16)


def products_kernel(row_ref, count_ref, basis_ref, stiff_from,
                    stiff_place_ref, stiff_shared_ref, basis_place_ref, pick_basis_ref,
                    pick, place, stiff, basis2, basis3, sems):
    copy = pltpu.make_async_copy(stiff_from, stiff, sems.at[0])
    copy.start()
    fill_pick(row_ref, pick)
    fill_place(row_ref, place)
    weight = 1.0 / count_ref[...].astype(F32)
    fill_basis2(basis_ref, basis2)
    scaled = basis2[...].astype(F32) * weight
    basis_place_ref[...] = dot(scaled.astype(BF16), place[...]).astype(BF16)
    fill_basis3(basis_ref, basis3)
    full = weights_of(count_ref)
    for left in range(0, basis3.shape[1], LANES):
        at = slice(left, left + LANES)
        basis3[:, at] = (basis3[:, at].astype(F32) * full).astype(BF16)
    for lo, n in tiles(pick.shape[0]):
        pick_basis_ref[lo : lo + n, :] = dot(pick[lo : lo + n, :], basis3[...]).astype(BF16)
    copy.wait()

    def product(lo):
        at = pl.ds(lo, FINE)
        stiff_place_ref[at, :] = dot(stiff[at, :], place[...]).astype(BF16)

    def shared(lo):
        at = pl.ds(lo, FINE)
        stiff_shared_ref[at, :] = dot(pick[at, :], stiff_place_ref[...]).astype(BF16)

    each(stiff.shape[0], FINE, product)
    each(pick.shape[0], FINE, shared)


def local_products_kernel(row_ref, count_ref, after_ref, inverse_from, local_place_ref,
                          place, inverse, sems):
    copies = bring([(inverse_from, inverse)], sems)
    fill_place(row_ref, place)
    rows = place.shape[0]
    weight = jnp.broadcast_to(1.0 / count_ref[...].astype(F32), (8, rows)).astype(BF16)
    listed = dot(weight, place[...])[0:1]
    for copy in copies:
        copy.wait()

    def product(lo):
        at = pl.ds(lo, FINE)
        local_place_ref[at, :] = (dot(inverse[at, :], place[...]) * listed).astype(BF16)

    each(rows, FINE, product)


def shared_products_kernel(local_place_ref, after_ref, pick_ref, weight_ref, local_shared_ref):
    slots = pick_ref.shape[0]
    weight = weight_ref[...].astype(BF16)

    def some(lo):
        at = pl.ds(lo, FINE)
        shared = dot(pick_ref[at, :], local_place_ref[...])
        turned = dot(pick_ref[at, :], weight)
        for left in range(0, slots, LANES):
            scaled = shared[:, left : left + LANES] * turned
            local_shared_ref[at, left : left + LANES] = scaled.astype(BF16)

    each(slots, FINE, some)


def tables_kernel(row_ref, count_ref, basis_ref, after_ref, stiff_from, stiff_place_from,
                  stiff_shared_from,
                  pick_ref, place_ref, weight_ref, basis2_ref, basis3_ref,
                  stiff_ref, stiff_place_ref, stiff_shared_ref, sems):
    copies = bring(
        [
            (stiff_from, stiff_ref),
            (stiff_shared_from, stiff_shared_ref),
            (stiff_place_from, stiff_place_ref),
        ],
        sems,
    )
    fill_pick(row_ref, pick_ref)
    fill_place(row_ref, place_ref)
    weight_ref[...] = weights_of(count_ref)
    fill_basis2(basis_ref, basis2_ref)
    fill_basis3(basis_ref, basis3_ref)
    for copy in copies:
        copy.wait()


def small_kernel(after_ref, first_from, second_from, first_ref, second_ref, sems):
    for copy in bring([(first_from, first_ref), (second_from, second_ref)], sems):
        copy.wait()


def columns_kernel(map_ref, inverse_from, out_ref, turned, rows, sems):
    parts = rows.shape[0]
    width = rows.shape[2]
    copies = bring(
        [(inverse_from.at[:, pl.ds(k * width, width)], rows.at[k]) for k in range(parts)], sems
    )
    for k in range(parts):
        copies[k].wait()
        turned[k * width : (k + 1) * width, :] = rows[k].T
    size = map_ref.shape[0]
    ncl = out_ref.shape[0] // size

    def step(i, _):
        for k in range(ncl):
            out_ref[pl.ds(i * ncl + k, 1), :] = turned[pl.ds(map_ref[i, k], 1), :]
        return 0

    lax.fori_loop(0, size, step, 0)


def coarse_kernel(map_ref, which_ref, got_ref, keep_ref, send_ref, turned, rowed):
    ncl, half = keep_ref.shape
    width = got_ref.shape[1]
    fill = jnp.zeros((turned.shape[1] - ncl, width), F32)
    for t in range(got_ref.shape[0] // ncl):
        block = jnp.concatenate([got_ref[t * ncl : (t + 1) * ncl, :], fill], axis=0)
        turned[t * width : (t + 1) * width, :] = block.T

    size = map_ref.shape[0]

    def step(i, _):
        for c in range(2):
            for k in range(ncl):
                row = turned[pl.ds(map_ref[2 * i + c, k], 1), :]
                rowed[pl.ds(c * half + i * ncl + k, 1), :] = row
        return 0

    lax.fori_loop(0, size // 2, step, 0)
    first = rowed[:half, :].T[:ncl, :]
    second = rowed[half:, :].T[:ncl, :]
    even = which_ref[0] == 0
    keep_ref[...] = jnp.where(even, first, second)
    send_ref[...] = jnp.where(even, second, first)


def stack_kernel(own_ref, other_ref, terms_ref, out_ref, after_ref):
    after_ref[...] = jnp.zeros_like(after_ref)
    ncl = own_ref.shape[0]
    own_high, own_low = cut(own_ref[...])
    other_high, other_low = cut(other_ref[...])
    out_ref[:ncl, :] = own_high
    out_ref[ncl : 2 * ncl, :] = other_high
    out_ref[2 * ncl : 3 * ncl, :] = own_low
    out_ref[3 * ncl :, :] = other_low


def send_terms(terms, scalars, send_ref):
    block = jnp.concatenate([terms, scalars], axis=0)
    rows = block.shape[0]
    for g in range(send_ref.shape[0] // rows):
        send_ref[g * rows : (g + 1) * rows, :] = block


def front(inverse_ref, weight_ref, pick_ref, cat, local_ref, out_ref, cat2):
    def product(lo):
        at = pl.ds(lo, HALF)
        local = halves(dot(inverse_ref[at, :], cat[...]))
        local_ref[at, :] = local
        cat2[at, :] = pair(weight_ref[at, :] * local)

    def shared(lo):
        at = pl.ds(lo, SLOTS)
        out_ref[at, :] = halves(dot(pick_ref[at, :], cat2[...]))

    each(inverse_ref.shape[0], HALF, product)
    each(pick_ref.shape[0], SLOTS, shared)


def first_kernel(loads_ref, a0, a1, a2, a3, row_ref, count_ref, basis_ref, inverse_from,
                 resid_ref, local_ref, pre_ref, send_ref,
                 cat, arr_cat, place, pick, basis2, inverse, weight, cat2, sems):
    copy = pltpu.make_async_copy(inverse_from, inverse, sems.at[0])
    copy.start()
    fill_place(row_ref, place)
    fill_basis2(basis_ref, basis2)
    weight[...] = weights_of(count_ref)
    ncl, rhs = basis_ref.shape[0], loads_ref.shape[1]
    arrivals((a0, a1, a2, a3), arr_cat)
    terms = jnp.zeros((2 * ncl, 2 * rhs), F32)
    for lo, n in tiles(loads_ref.shape[0]):
        at = slice(lo, lo + n)
        resid = loads_ref[at, :] + halves(dot(place[at, :], arr_cat[...]))
        resid_ref[at, :] = resid
        both = pair(weight[at, :] * resid)
        cat[at, :] = both
        terms += dot(basis2[:, at], both)
    send_terms(three(terms, ncl), jnp.zeros((SCAL, rhs), F32), send_ref)
    fill_pick(row_ref, pick)
    copy.wait()
    front(inverse, weight, pick, cat, local_ref, pre_ref, cat2)


def coarse_solve_kernel(got_ref, g_ref, own_ref, other_ref):
    ncl = g_ref.shape[0] // 4
    rows = ncl + SCAL
    groups = got_ref.shape[0] // rows
    got = got_ref[...].reshape(groups, rows, got_ref.shape[1])
    terms = got[:, :ncl].reshape(groups * ncl, got_ref.shape[1])
    scalars = jnp.sum(got[:, ncl:], axis=0)
    values = three(dot(g_ref[...], pair(terms)), 2 * ncl)
    own_ref[:ncl, :] = values[:ncl]
    own_ref[ncl:, :] = scalars
    other_ref[:ncl, :] = values[ncl:]
    other_ref[ncl:, :] = scalars


def back_kernel(own_ref, other_ref, pre_ref, pick_basis_ref,
                values_ref, scal_ref, out0, out1, out2, out3):
    ncl = own_ref.shape[0] - SCAL
    total = own_ref[...] + other_ref[...]
    scal_ref[...] = total[ncl:]
    high, low = cut(total[:ncl])
    fill = jnp.zeros((values_ref.shape[0] - 3 * ncl, high.shape[1]), BF16)
    values = jnp.concatenate([high, low, high, fill], axis=0)
    values_ref[...] = values
    cap = out0.shape[0]
    for j, out in enumerate((out0, out1, out2, out3)):
        at = slice(j * cap, (j + 1) * cap)
        out[...] = pre_ref[at, :] + dot(pick_basis_ref[at, :], values)


def part_kernel(flat, values_ref, local_ref, weight_ref, basis3_ref, stiff_ref, pick_ref,
                part_ref, image_ref, pre_ref, cat, cat2):
    values = values_ref[...]
    small, large, shared_step = (FINE, FINE, FINE) if flat else (TILE, HALF, SLOTS)

    def field(lo):
        at = pl.ds(lo, small)
        part = weight_ref[at, :] * (local_ref[at, :] + dot(basis3_ref[at, :], values))
        part_ref[at, :] = part
        cat[at, :] = pair(part)

    def product(lo):
        at = pl.ds(lo, large)
        image = halves(dot(stiff_ref[at, :], cat[...]))
        image_ref[at, :] = image
        cat2[at, :] = pair(image)

    def shared(lo):
        at = pl.ds(lo, shared_step)
        pre_ref[at, :] = halves(dot(pick_ref[at, :], cat2[...]))

    each(local_ref.shape[0], small, field, flat)
    each(local_ref.shape[0], large, product, flat)
    each(pick_ref.shape[0], shared_step, shared, flat)


def shared_kernel(a0, a1, a2, a3, pre_ref, stiff_shared_ref,
                  arr_ref, out0, out1, out2, out3):
    arrivals((a0, a1, a2, a3), arr_ref)
    cap = out0.shape[0]
    for j, out in enumerate((out0, out1, out2, out3)):
        at = slice(j * cap, (j + 1) * cap)
        out[...] = pre_ref[at, :] + halves(dot(stiff_shared_ref[at, :], arr_ref[...]))


def completed(ref, at, table_ref, arr_ref):
    return ref[at, :] + halves(dot(table_ref[at, :], arr_ref[...]))


def collect(sums, rhs):
    rows = [jnp.sum(s, axis=0, keepdims=True) for s in sums]
    rows.append(jnp.zeros((SCAL - len(rows), rhs), F32))
    return jnp.concatenate(rows, axis=0)


def start_kernel(part_ref, image_ref, arr_ref, r_ref, place_ref, stiff_place_ref,
                 weight_ref, basis2_ref, inverse_from, local_place_from,
                 u_ref, w_ref, terms_ref, sums_ref,
                 inverse_ref, local_place_ref, sems):
    copies = bring(
        [
            (inverse_from, inverse_ref),
            (local_place_from, local_place_ref),
        ],
        sems,
    )
    ncl = basis2_ref.shape[0] // 2
    rhs = r_ref.shape[1]

    def some(lo, carry):
        ru, uw, terms = carry
        at = pl.ds(lo, TILE)
        u = completed(part_ref, at, place_ref, arr_ref)
        w = completed(image_ref, at, stiff_place_ref, arr_ref)
        u_ref[at, :] = u
        w_ref[at, :] = w
        weight = weight_ref[at, :]
        ru += folded(weight * u * r_ref[at, :])
        uw += folded(u * w)
        return ru, uw, terms + dot(basis2_ref[:, at], pair(weight * w))

    zero = jnp.zeros((8, rhs), F32)
    start = (zero, zero, jnp.zeros((2 * ncl, 2 * rhs), F32))
    *sums, terms = summed(r_ref.shape[0], TILE, some, start)
    terms_ref[...] = three(terms, ncl)
    sums_ref[...] = collect(sums, rhs)
    for copy in copies:
        copy.wait()


def second_kernel(part_ref, image_ref, arr_ref, scal_ref, r_ref, u_ref, w_ref,
                  place_ref, stiff_place_ref, weight_ref, basis2_ref,
                  m_ref, z_ref, x1_ref, r1_ref, u1_ref, w1_ref, terms_ref, sums_ref):
    ncl = basis2_ref.shape[0] // 2
    rhs = r_ref.shape[1]
    alpha = scal_ref[0:1, :] / scal_ref[1:2, :]

    def some(lo, carry):
        *sums, terms = carry
        at = pl.ds(lo, TILE)
        m = completed(part_ref, at, place_ref, arr_ref)
        z = completed(image_ref, at, stiff_place_ref, arr_ref)
        m_ref[at, :] = m
        z_ref[at, :] = z
        weight = weight_ref[at, :]
        p, s = u_ref[at, :], w_ref[at, :]
        x1_ref[at, :] = alpha * p
        r1 = r_ref[at, :] - alpha * s
        u1 = p - alpha * m
        w1 = s - alpha * z
        r1_ref[at, :] = r1
        u1_ref[at, :] = u1
        w1_ref[at, :] = w1
        left = weight * s - alpha * z
        weighted = weight * u1
        news = (weighted * r1, u1 * left, weighted * s, p * left)
        sums = [old + folded(new) for old, new in zip(sums, news)]
        return *sums, terms + dot(basis2_ref[:, at], pair(weight * w1))

    start = (jnp.zeros((8, rhs), F32),) * 4 + (jnp.zeros((2 * ncl, 2 * rhs), F32),)
    *sums, terms = summed(r_ref.shape[0], TILE, some, start)
    terms_ref[...] = three(terms, ncl)
    sums_ref[...] = collect(sums, rhs)


def terms_kernel(a0, a1, a2, a3, terms_ref, sums_ref, basis_place_ref, *refs):
    *scal, arr_ref, send_ref = refs
    ncl = terms_ref.shape[0]
    arrivals((a0, a1, a2, a3), arr_ref)
    added = three(dot(basis_place_ref[...], arr_ref[...]), ncl)
    if scal:
        added *= -scal[0][0:1, :] / scal[0][1:2, :]
    send_terms(terms_ref[...] + added, sums_ref[...], send_ref)


def local_part_kernel(w_ref, weight_ref, inverse_ref, pick_ref, local_ref, pre_ref, cat, cat2):
    for lo, n in tiles(w_ref.shape[0], FINE):
        at = slice(lo, lo + n)
        cat[at, :] = pair(weight_ref[at, :] * w_ref[at, :])
    front(inverse_ref, weight_ref, pick_ref, cat, local_ref, pre_ref, cat2)


def local_shared_kernel(pre_ref, arr_ref, after_ref, local_shared_ref, scal_ref, out_ref):
    factor = -scal_ref[0:1, :] / scal_ref[1:2, :]
    for lo, n in tiles(pre_ref.shape[0]):
        at = slice(lo, lo + n)
        came = halves(dot(local_shared_ref[at, :], arr_ref[...]))
        out_ref[at, :] = pre_ref[at, :] + factor * came


def local_again_kernel(pre_ref, arr_ref, after_ref, local_place_ref, weight_ref, pick_ref,
                       out_ref, cat):
    for lo, n in tiles(weight_ref.shape[0], FINE):
        at = slice(lo, lo + n)
        came = halves(dot(local_place_ref[at, :], arr_ref[...]))
        cat[at, :] = pair(weight_ref[at, :] * came)
    for lo, n in tiles(pre_ref.shape[0], FINE):
        at = slice(lo, lo + n)
        out_ref[at, :] = pre_ref[at, :] + halves(dot(pick_ref[at, :], cat[...]))


def complete_kernel(w_part_ref, local_part_ref, arr_ref, after_ref, place_ref, local_place_ref,
                    *refs):
    *more, w_ref, local_ref = refs
    if more:
        scal_ref, z_part_ref, z_ref = more
        factor = -scal_ref[0:1, :] / scal_ref[1:2, :]

    def some(lo):
        at = pl.ds(lo, TILE)
        came = halves(dot(place_ref[at, :], arr_ref[...]))
        local = halves(dot(local_place_ref[at, :], arr_ref[...]))
        if more:
            z_ref[at, :] = z_part_ref[at, :] + came
            came, local = factor * came, factor * local
        w_ref[at, :] = w_part_ref[at, :] + came
        local_ref[at, :] = local_part_ref[at, :] + local

    each(w_ref.shape[0], TILE, some)


def step_scalars(before, now):
    beta = now[0:1, :] / before[0:1, :]
    energy = now[1:2, :] + beta * (now[2:3, :] + now[3:4, :]) + beta * beta * before[1:2, :]
    return beta, now[0:1, :] / energy, energy


def third_kernel(part_ref, image_ref, arr_ref, before_ref, scal_ref,
                 x1_ref, r1_ref, u1_ref, w1_ref, p_ref, s_ref, q_ref, z_ref,
                 place_ref, stiff_place_ref, weight_ref,
                 send_ref, state_ref, x2_ref, r2_ref, u2_ref, half_ref, p1_ref, s1_ref):
    rhs = r1_ref.shape[1]
    beta, alpha, energy = step_scalars(before_ref[...], scal_ref[...])

    def some(lo, sums):
        at = pl.ds(lo, TILE)
        m = completed(part_ref, at, place_ref, arr_ref)
        image = completed(image_ref, at, stiff_place_ref, arr_ref)
        p1 = u1_ref[at, :] + beta * p_ref[at, :]
        s1 = w1_ref[at, :] + beta * s_ref[at, :]
        q1 = m + beta * q_ref[at, :]
        r2 = r1_ref[at, :] - alpha * s1
        u2 = u1_ref[at, :] - alpha * q1
        half = w1_ref[at, :] - (alpha * beta) * z_ref[at, :]
        weight = weight_ref[at, :]
        left = weight * half - alpha * image
        weighted = weight * u2
        x2_ref[at, :] = x1_ref[at, :] + alpha * p1
        r2_ref[at, :] = r2
        u2_ref[at, :] = u2
        half_ref[at, :] = half - alpha * image
        p1_ref[at, :] = p1
        s1_ref[at, :] = s1
        news = (weighted * r2, u2 * left, weighted * s1, p1 * left)
        return tuple(old + folded(new) for old, new in zip(sums, news))

    sums = summed(r1_ref.shape[0], TILE, some, (jnp.zeros((8, rhs), F32),) * 4)
    block = collect(sums, rhs)
    for g in range(send_ref.shape[0] // SCAL):
        send_ref[g * SCAL : (g + 1) * SCAL, :] = block
    state_ref[...] = jnp.concatenate(
        [scal_ref[0:1, :], energy, alpha, jnp.zeros((SCAL - 3, rhs), F32)], axis=0
    )


def last_kernel(state_ref, got_ref, a0, a1, a2, a3, place_ref,
                x2, u2, p1, r2, half, s1,
                x3_to, r3_to, arr_cat, x3, r3, out_sems):
    state = state_ref[...]
    now = jnp.sum(got_ref[...].reshape(-1, SCAL, got_ref.shape[1]), axis=0)
    beta, alpha, _ = step_scalars(state, now)
    old = state[2:3, :]
    arrivals((a0, a1, a2, a3), arr_cat)
    outs = []
    for i, (lo, n) in enumerate(tiles(r2.shape[0])):
        at = slice(lo, lo + n)
        x3[at, :] = x2[at, :] + alpha * (u2[at, :] + beta * p1[at, :])
        w2 = half[at, :] - old * halves(dot(place_ref[at, :], arr_cat[...]))
        r3[at, :] = r2[at, :] - alpha * (w2 + beta * s1[at, :])
        rows = pl.ds(lo, n)
        outs += bring(
            [(x3.at[rows, :], x3_to.at[rows, :]), (r3.at[rows, :], r3_to.at[rows, :])],
            out_sems.at[i],
        )
    for copy in outs:
        copy.wait()


def body(
    stiffness, local_inverse, coarse_basis, loads, counts, shared_rows, coarse_map, coarse_inverse
):
    size = lax.axis_size("sub")
    me = lax.axis_index("sub")
    rows, rhs = loads.shape[1:]
    ncl = coarse_basis.shape[1]
    slots, cap = shared_rows.shape[1:]
    order = coarse_inverse.shape[1]
    lists = slots * cap
    stiff, inverse = aside(stiffness[0], local_inverse[0])

    def partner(distance, parity):
        def of(i):
            up = (i // distance) % 2 == parity
            return (i + distance if up else i - distance) % size

        return [(i, of(i)) for i in range(size)]

    inside = partner(1, 0)
    swaps = [inside, partner(1, 1), partner(STRIDE, 0), partner(STRIDE, 1)]
    swaps = [swaps[j] for j in ORDER]

    def exchange(outs):
        return [lax.ppermute(out, "sub", swap) for out, swap in zip(outs, swaps)]

    cores = [[2 * i + c for i in range(size // 2)] for c in range(2)]
    groups = size // 2
    block = ncl + SCAL

    fields = (rows, rhs)
    out4 = [far((cap, rhs))] * 4
    wide = pltpu.VMEM((rows, 2 * rhs), BF16)
    wide_arr = pltpu.VMEM((lists, 2 * rhs), BF16)
    place_like = pltpu.VMEM((rows, lists), BF16)
    pick_like = pltpu.VMEM((lists, rows), BF16)
    basis = coarse_basis[0]
    (loads_aside,) = aside(loads[0])

    listed, *outs = call(
        loads_kernel,
        "loads",
        (shared_rows[0], loads_aside),
        [far((1, lists), jnp.int32)] + out4,
        [pick_like, wide, pltpu.VMEM(fields, F32), pltpu.SemaphoreType.DMA((1,))],
        {1: ASPEC},
    )
    arrived = exchange(outs)
    own_map = jnp.pad(coarse_map, ((0, 0), (0, -ncl % LANES)))
    maps = jnp.broadcast_to(own_map, (size, own_map.shape[1]))
    maps = lax.all_to_all(maps, "sub", 0, 0, tiled=True)
    maps, *arrived = lax.optimization_barrier((maps, *arrived))


    (picked,) = call(
        columns_kernel,
        "coarse_columns",
        (maps, *aside(coarse_inverse)),
        [far((size * ncl, coarse_inverse.shape[0]))],
        [
            pltpu.VMEM((order, coarse_inverse.shape[0]), F32),
            pltpu.VMEM((4, coarse_inverse.shape[0], order // 4), F32),
            pltpu.SemaphoreType.DMA((4,)),
        ],
        {0: SSPEC, 1: ASPEC},
        mib=30,
    )
    mine_rows = lax.all_to_all(picked, "sub", 0, 0, tiled=True)

    r0, local, pre, send = call(
        first_kernel,
        "residual_and_terms",
        (loads[0], *arrived, listed, counts, basis, inverse),
        [away(fields), away(fields), away((lists, rhs)), far((groups * block, rhs))],
        [
            wide,
            wide_arr,
            place_like,
            pick_like,
            pltpu.VMEM((2 * ncl, rows), BF16),
            pltpu.VMEM((rows, rows), BF16),
            pltpu.VMEM(fields, F32),
            wide,
            pltpu.SemaphoreType.DMA((1,)),
        ],
        {8: ASPEC},
        us=6,
        mib=30,
    )
    products = call(
        products_kernel,
        "products",
        (listed, counts, basis, stiff),
        [
            away((rows, lists), BF16),
            away((lists, lists), BF16),
            away((2 * ncl, lists), BF16),
            away((lists, 2 * LANES), BF16),
        ],
        [
            pick_like,
            place_like,
            pltpu.VMEM((rows, rows), BF16),
            pltpu.VMEM((2 * ncl, rows), BF16),
            pltpu.VMEM((rows, 2 * LANES), BF16),
            pltpu.SemaphoreType.DMA((1,)),
        ],
        {3: ASPEC},
        us=10,
        mib=30,
    )
    r0, local, pre = aside(r0, local, pre)

    keep, pass_on = call(
        coarse_kernel,
        "coarse_block",
        (maps, (me % 2).reshape(1), mine_rows),
        [far((ncl, groups * ncl)), far((ncl, groups * ncl))],
        [
            pltpu.VMEM((order, LANES), F32),
            pltpu.VMEM((size * ncl, LANES), F32),
        ],
        {0: SSPEC, 1: SSPEC},
        mib=30,
    )
    passed = lax.ppermute(pass_on, "sub", inside)

    def share(send):
        return lax.all_to_all(send, "sub", 0, 0, tiled=True, axis_index_groups=cores)

    send, *products = lax.optimization_barrier((send, *products))
    terms = share(send)
    local_products = call(
        local_products_kernel,
        "local_products",
        (listed, counts, send, inverse),
        [away((rows, lists), BF16)],
        [place_like, pltpu.VMEM((rows, rows), BF16), pltpu.SemaphoreType.DMA((1,))],
        {2: ASPEC, 3: ASPEC},
        us=10,
        mib=30,
    )
    terms, *local_products = lax.optimization_barrier((terms, *local_products))
    local_products = aside(*local_products)
    coarse, after = call(
        stack_kernel,
        "coarse_addends",
        (keep, passed, terms),
        [near((4 * ncl, groups * ncl), BF16), far((SCAL, LANES))],
    )
    stiff_place, stiff_shared, basis_place, pick_basis = aside(*products)
    tables = held(*call(
        tables_kernel,
        "tables",
        (listed, counts, basis, after, stiff, stiff_place, stiff_shared),
        [
            near((lists, rows), BF16),
            near((rows, lists), BF16),
            near(fields),
            near((2 * ncl, rows), BF16),
            near((rows, 2 * LANES), BF16),
            near((rows, rows), BF16),
            near((rows, lists), BF16),
            near((lists, lists), BF16),
        ],
        [pltpu.SemaphoreType.DMA((3,))],
        {4: ASPEC, 5: ASPEC, 6: ASPEC},
        us=5,
    ))
    pick, place, weight, basis2, basis3, stiff, stiff_place, stiff_shared = tables
    tables = []
    (coarse,) = held(coarse)

    def correct(terms, pre, bring_in=None):
        own, other = call(
            coarse_solve_kernel,
            "coarse_solve",
            (terms, coarse),
            [far((block, rhs)), far((block, rhs))],
            us=1,
        )
        came = lax.ppermute(other, "sub", inside)
        if bring_in:
            small.extend(bring_in(own))
        values, scal, *outs = call(
            back_kernel,
            "coarse_back",
            (own, came, pre(own), small[0]),
            [near((2 * LANES, rhs), BF16), far((SCAL, rhs))] + out4,
            us=1,
        )
        return *held(values), scal, exchange(outs)

    small = []

    def bring_small(own):
        return held(*call(
            small_kernel,
            "small_tables",
            (own, pick_basis, basis_place),
            [near(pick_basis.shape, BF16), near(basis_place.shape, BF16)],
            [pltpu.SemaphoreType.DMA((2,))],
            {1: ASPEC, 2: ASPEC},
            us=1,
        ))

    def operate(values, local, arrived, *beside):
        part, image, pre = held(*call(
            functools.partial(part_kernel, not tables),
            "field_part",
            (values, local, weight, basis3, stiff, pick),
            [near(fields), near(fields), near((lists, rhs))],
            [wide, wide],
            us=3,
        ))
        if beside:
            pre, table = held(*lax.optimization_barrier((pre, *beside)))
            tables.append(table)
        arr, *outs = call(
            shared_kernel,
            "image_shared",
            (*arrived, pre, stiff_shared),
            [near((lists, 2 * rhs), BF16)] + out4,
            us=1,
        )
        return part, image, *held(arr), exchange(outs)

    def share_terms(arrived, terms, sums, *scal):
        arr, send = call(
            terms_kernel,
            "terms",
            (*arrived, terms, sums, small[1], *scal),
            [near((lists, 2 * rhs), BF16), far((groups * block, rhs))],
            us=1,
        )
        return *held(arr), share(send)

    def local_part(w):
        return held(*call(
            local_part_kernel,
            "local_part",
            (w, weight, inverse, pick),
            [near(fields), near((lists, rhs))],
            [wide, wide],
            us=3,
        ))

    def local_shared(pre, arr, scal):
        def of(own):
            return held(*call(
                local_shared_kernel,
                "local_shared",
                (pre, arr, own, shared_table, scal),
                [near((lists, rhs))],
                us=1,
            ))[0]

        return of

    def local_again(pre, arr):
        def of(own):
            return held(*call(
                local_again_kernel,
                "local_again",
                (pre, arr, own, local_place, weight, pick),
                [near((lists, rhs))],
                [wide],
                us=1,
            ))[0]

        return of

    def complete(w, local, arr, after, *more):
        return held(*call(
            complete_kernel,
            "complete",
            (w, local, arr, after, place, local_place, *more),
            [near(fields)] * (3 if more else 2),
            us=2,
        ))

    values, _, arrived = correct(terms, lambda own: pre, bring_small)
    part, image, arr, arrived = operate(values, local, arrived)
    tables.append(None)
    u0, w0, terms, sums, inverse, local_place = held(*call(
        start_kernel,
        "start",
        (part, image, arr, r0, place, stiff_place, weight, basis2, inverse, *local_products),
        [near(fields), near(fields), near((ncl, rhs)), near((SCAL, rhs))]
        + [near((rows, rows), BF16), near((rows, lists), BF16)],
        [pltpu.SemaphoreType.DMA((2,))],
        {8: ASPEC, 9: ASPEC},
        us=3,
    ))
    local, pre = local_part(w0)
    terms, pre = held(*lax.optimization_barrier((terms, pre)))
    arr, terms = share_terms(arrived, terms, sums)
    values, scal0, arrived = correct(terms, local_again(pre, arr))
    w0, local = complete(w0, local, arr, values)
    (shared_table,) = held(*call(
        shared_products_kernel,
        "shared_products",
        (local_place, values, pick, weight),
        [near((lists, lists), BF16)],
        us=4,
    ))

    part, image, arr, arrived = operate(values, local, arrived, shared_table)
    shared_table = tables[-1]
    m0, z0, x1, r1, u1, w1, terms, sums = held(*call(
        second_kernel,
        "first_update",
        (part, image, arr, scal0, r0, u0, w0, place, stiff_place, weight, basis2),
        [near(fields)] * 6 + [near((ncl, rhs)), near((SCAL, rhs))],
        us=4,
    ))
    local, pre = local_part(w1)
    terms, pre = held(*lax.optimization_barrier((terms, pre)))
    arr, terms = share_terms(arrived, terms, sums, scal0)
    values, scal1, arrived = correct(terms, local_shared(pre, arr, scal0))
    z0, w1, local = complete(w1, local, arr, values, scal0, z0)

    part, image, arr, arrived = operate(values, local, arrived)
    pieces = len(tiles(rows))
    send, state, *news = call(
        third_kernel,
        "second_update",
        (part, image, arr, scal0, scal1, x1, r1, u1, w1, u0, w0, m0, z0)
        + (place, stiff_place, weight),
        [far((size * SCAL, rhs)), far((SCAL, rhs))] + [near(fields)] * 6,
        us=4,
    )
    x2, r2, u2, half, p1, s1 = held(*news)
    send, *arrived = lax.optimization_barrier((send, *arrived))
    sums = lax.all_to_all(send, "sub", 0, 0, tiled=True)
    sums, *arrived = lax.optimization_barrier((sums, *arrived))
    x3, r3 = call(
        last_kernel,
        "last_update",
        (state, sums, *arrived, place, x2, u2, p1, r2, half, s1),
        [far(fields), far(fields)],
        [wide_arr, pltpu.VMEM(fields, F32), pltpu.VMEM(fields, F32)]
        + [pltpu.SemaphoreType.DMA((pieces, 2))],
        sent=range(2),
    )
    return (x3[None], r3[None])


def solution(mesh):
    placed = (
        P("sub", None, None),
        P("sub", None, None),
        P("sub", None, None),
        P("sub", None, None),
        P("sub", None),
        P("sub", None, None),
        P("sub", None),
        P("sub", None),
    )
    return jax.shard_map(
        body,
        mesh=mesh,
        in_specs=placed,
        out_specs=(P("sub", None, None), P("sub", None, None)),
        check_vma=False,
    )
```

profile of v0, /device:TPU:0, one launch (start us, length us, event | category | flops | bytes accessed | tf_op | source)
XLA Modules:
  0.0 207.7 jit_solution(10613797832781812502)
XLA Ops:
  3.6 5.1 %collective-permute-start = (f32[256,128]{1,0:T(8,128)S(1)}, f32[256,128]{1,0:T(8,128)S(1)}, u32[]{:S(2)}, u32[]{:S(2)}) collective-permute-start(f32[256,128]{1,0:T(8,128)S(1)} %get-tuple-element.141), channel_id=1, source_target_pairs={{0,24},{1,25},{2,26},{3,27},{4,28},{5,29},{6,30},{7,31},{8,16},{9,... | collective-permute-start | bytes 393224 | tf_op jit(solution)/shard_map/ppermute | solution.py:682
  12.5 10.3 %all_to_all.66 = s32[32,1,128]{2,1,0:T(1,128)S(1)} all-to-all(s32[32,1,128]{2,1,0:T(1,128)S(1)} %broadcast_in_dim.11), channel_id=1, replica_groups=mesh['sub'=32] {'sub'}, dimensions={0} | all-to-all | bytes 32768 | tf_op jit(solution)/shard_map/all_to_all | solution.py:708
  22.8 5.0 %coarse_columns.1 = f32[1536,128]{1,0:T(8,128)} custom-call(s32[32,128]{1,0:T(8,128)S(1)} %bitcast.34, f32[128,4096]{1,0:T(8,128)} %inverse_from.1), custom_call_target="tpu_custom_call" | custom-call | bytes 6000000 | tf_op jit(solution)/shard_map/coarse_columns/pallas_call | solution.py:48
  27.7 2.8 %all-to-all-start.2 = ((f32[32,48,128]{2,1,0:T(8,128)}), f32[32,48,128]{2,1,0:T(8,128)S(1)}, u32[]{:S(2)}, u32[]{:S(2)}) async-start(f32[32,48,128]{2,1,0:T(8,128)} %bitcast.10), calls=%async_computation.2 | async-start | bytes 1572864 | tf_op jit(solution)/shard_map/all_to_all | solution.py:725
  30.5 14.7 %products.1 = (bf16[1536,1024]{1,0:T(8,128)(2,1)}, bf16[1024,1024]{1,0:T(8,128)(2,1)}, bf16[96,1024]{1,0:T(8,128)(2,1)}, bf16[1024,256]{1,0:T(8,128)(2,1)}) custom-call(s32[1,1024]{1,0:T(1,128)S(1)} %get-tuple-element.149.row_ref, s32[1,1536]{1,0:T(1,128)S(1)} %copy-done.2, f32[48,1536]{1,0:T(8,128)S(1)} %bitcast.26, bf16[1536,1536]{1,0:T(8,128)(2,1)} %bitcast.41), custom_call_target="tpu_custom_call" | custom-call | bytes 30000000 | tf_op jit(solution)/shard_map/products/pallas_call | solution.py:48
  45.3 6.7 %residual_and_terms.1 = (f32[1536,128]{1,0:T(8,128)}, f32[1536,128]{1,0:T(8,128)}, f32[1024,128]{1,0:T(8,128)}, f32[896,128]{1,0:T(8,128)}) custom-call(f32[1536,128]{1,0:T(8,128)S(1)} %bitcast.25, f32[256,128]{1,0:T(8,128)S(1)} %collective-permute-done.a0, f32[256,128]{1,0:T(8,128)S(1)} %collective-permute-done.1.a1, ...), custom_call_target="tpu_custom_call" | custom-call | bytes 18000000 | tf_op jit(solution)/shard_map/residual_and_terms/pallas_call | solution.py:48
  52.0 6.9 %all-to-all-start.1 = ((f32[16,56,128]{2,1,0:T(8,128)}), f32[16,56,128]{2,1,0:T(8,128)S(1)}, u32[]{:S(2)}, u32[]{:S(2)}) async-start(f32[16,56,128]{2,1,0:T(8,128)} %bitcast.7), calls=%async_computation.1 | async-start | bytes 917504 | tf_op jit(solution)/shard_map/all_to_all | solution.py:786
  58.9 2.9 %coarse_block.1 = (f32[48,768]{1,0:T(8,128)S(1)}, f32[48,768]{1,0:T(8,128)S(1)}) custom-call(s32[32,128]{1,0:T(8,128)S(1)} %bitcast.35, s32[1]{0:T(128)} %bitcast.9.which_ref, f32[1536,128]{1,0:T(8,128)S(1)} %bitcast.23), custom_call_target="tpu_custom_call" | custom-call | bytes 6000000 | tf_op jit(solution)/shard_map/coarse_block/pallas_call | solution.py:48
  61.9 9.9 %local_products.1.local_place_from = bf16[1536,1024]{1,0:T(8,128)(2,1)} custom-call(s32[1,1024]{1,0:T(1,128)S(1)} %get-tuple-element.149.row_ref, s32[1,1536]{1,0:T(1,128)S(1)} %copy-done.2, f32[896,128]{1,0:T(8,128)} %get-tuple-element.155.after_ref, bf16[1536,1536]{1,0:T(8,128)(2,1)} %bitcast.39), custom_call_target="tpu_custom_call" | custom-call | bytes 30000000 | tf_op jit(solution)/shard_map/local_products/pallas_call | solution.py:48
  76.4 2.9 %collective-permute-start.6 = (f32[256,128]{1,0:T(8,128)S(1)}, f32[256,128]{1,0:T(8,128)S(1)}, u32[]{:S(2)}, u32[]{:S(2)}) collective-permute-start(f32[256,128]{1,0:T(8,128)S(1)} %get-tuple-element.167), channel_id=1, source_target_pairs={{0,24},{1,25},{2,26},{3,27},{4,28},{5,29},{6,30},{7,31},{8,16},{9,... | collective-permute-start | bytes 393224 | tf_op jit(solution)/shard_map/ppermute | solution.py:682
  82.6 4.0 %tables.1 = (bf16[1024,1536]{1,0:T(8,128)(2,1)S(1)}, bf16[1536,1024]{1,0:T(8,128)(2,1)S(1)}, f32[1536,128]{1,0:T(8,128)S(1)}, bf16[96,1536]{1,0:T(8,128)(2,1)S(1...) custom-call(s32[1,1024]{1,0:T(1,128)S(1)} %get-tuple-element.149.row, ...), custom_call_target="tpu_custom_call" | custom-call | bytes 15000000 | tf_op jit(solution)/shard_map/tables/pallas_call | solution.py:48
  86.6 3.6 %field_part.3 = (f32[1536,128]{1,0:T(8,128)S(1)}, f32[1536,128]{1,0:T(8,128)S(1)}, f32[1024,128]{1,0:T(8,128)S(1)}) custom-call(bf16[256,128]{1,0:T(8,128)(2,1)S(1)} %get-tuple-element.171.values_ref, f32[1536,128]{1,0:T(8,128)} %get-tuple-element.172.local_ref, f32[1536,128]{1,0:T(8,128)S(1)} %get-tuple-element.176.weight_ref, ...), custom_call_target="tpu_custom_call" | custom-call | bytes 9000000 | tf_op jit(solution)/shard_map/field_part/pallas_call | solution.py:48
  94.8 4.5 %start.1 = (f32[1536,128]{1,0:T(8,128)S(1)}, f32[1536,128]{1,0:T(8,128)S(1)}, f32[48,128]{1,0:T(8,128)S(1)}, f32[8,128]{1,0:T(8,128)S(1)}, bf16[1536,1536]{1,0:T...) custom-call(f32[1536,128]{1,0:T(8,128)S(1)} %get-tuple-element.186.part_ref, f32[1536,128]{1,0:T(8,128)S(1)} %get-tuple-element.187.image_ref, ...), custom_call_target="tpu_custom_call" | custom-call | bytes 9000000 | tf_op jit(solution)/shard_map/start/pallas_call | solution.py:48
  99.3 2.8 %local_part.2 = (f32[1536,128]{1,0:T(8,128)S(1)}, f32[1024,128]{1,0:T(8,128)S(1)}) custom-call(f32[1536,128]{1,0:T(8,128)S(1)} %get-tuple-element.195.w_ref.w_part_ref, f32[1536,128]{1,0:T(8,128)S(1)} %get-tuple-element.176.weight_ref, bf16[1536,1536]{1,0:T(8,128)(2,1)S(1)} %get-tuple-element.196.inverse_ref, bf16[1024,1536]{1,0:T(8,128)(2,1)S(1)} %get-tuple-element.179.pick_ref), custom_call_target="tpu_custom_call" | custom-call | bytes 9000000 | tf_op jit(solution)/shard_map/local_part/pallas_call | solution.py:48
  102.5 18.8 %all_to_all.67 = f32[16,56,128]{2,1,0:T(8,128)S(1)} all-to-all(f32[16,56,128]{2,1,0:T(8,128)S(1)} %bitcast.33), channel_id=1, replica_groups={{0,2,4,6,8,10,12,14,16,18,20,22,24,26,28,30},{1,3,5,7,9,11,13,15,17,19,..., dimensions={0} | all-to-all | bytes 917504 | tf_op jit(solution)/shard_map/all_to_all | solution.py:786
  128.0 5.0 %shared_products.1.local_shared_ref = bf16[1024,1024]{1,0:T(8,128)(2,1)S(1)} custom-call(bf16[1536,1024]{1,0:T(8,128)(2,1)S(1)} %get-tuple-element.206.local_place_ref, bf16[256,128]{1,0:T(8,128)(2,1)S(1)} %get-tuple-element.211.after_ref.values_ref, bf16[1024,1536]{1,0:T(8,128)(2,1)S(1)} %get-tuple-element.179.pick_ref, ...), custom_call_target="tpu_custom_call" | custom-call | bytes 12000000 | tf_op jit(solution)/shard_map/shared_products/pallas_call | solution.py:48
  135.2 3.4 %field_part.4 = (f32[1536,128]{1,0:T(8,128)S(1)}, f32[1536,128]{1,0:T(8,128)S(1)}, f32[1024,128]{1,0:T(8,128)S(1)}) custom-call(bf16[256,128]{1,0:T(8,128)(2,1)S(1)} %get-tuple-element.211.after_ref.values_ref, f32[1536,128]{1,0:T(8,128)S(1)} %get-tuple-element.213.local_ref, f32[1536,128]{1,0:T(8,128)S(1)} %get-tuple-element.176.weight_ref, ...), custom_call_target="tpu_custom_call" | custom-call | bytes 9000000 | tf_op jit(solution)/shard_map/field_part/pallas_call | solution.py:48
  139.8 3.4 %collective-permute-start.20 = (f32[256,128]{1,0:T(8,128)S(1)}, f32[256,128]{1,0:T(8,128)S(1)}, u32[]{:S(2)}, u32[]{:S(2)}) collective-permute-start(f32[256,128]{1,0:T(8,128)S(1)} %get-tuple-element.217), channel_id=1, source_target_pairs={{0,31},{1,2},{2,1},{3,4},{4,3},{5,6},{6,5},{7,8},{8,7},{9,10},{10,... | collective-permute-start | bytes 393224 | tf_op jit(solution)/shard_map/ppermute | solution.py:682
  144.1 4.1 %first_update.1 = (f32[1536,128]{1,0:T(8,128)S(1)}, f32[1536,128]{1,0:T(8,128)S(1)}, f32[1536,128]{1,0:T(8,128)S(1)}, f32[1536,128]{1,0:T(8,128)S(1)}, f32[1536,...) custom-call(f32[1536,128]{1,0:T(8,128)S(1)} %get-tuple-element.220.part_ref, ...), custom_call_target="tpu_custom_call" | custom-call | bytes 12000000 | tf_op jit(solution)/shard_map/first_update/pallas_call | solution.py:48
  148.2 2.9 %local_part.3 = (f32[1536,128]{1,0:T(8,128)S(1)}, f32[1024,128]{1,0:T(8,128)S(1)}) custom-call(f32[1536,128]{1,0:T(8,128)S(1)} %get-tuple-element.227.w_ref.w_part_ref, f32[1536,128]{1,0:T(8,128)S(1)} %get-tuple-element.176.weight_ref, bf16[1536,1536]{1,0:T(8,128)(2,1)S(1)} %get-tuple-element.196.inverse_ref, bf16[1024,1536]{1,0:T(8,128)(2,1)S(1)} %get-tuple-element.179.pick_ref), custom_call_target="tpu_custom_call" | custom-call | bytes 9000000 | tf_op jit(solution)/shard_map/local_part/pallas_call | solution.py:48
  151.5 18.0 %all_to_all.68 = f32[16,56,128]{2,1,0:T(8,128)S(1)} all-to-all(f32[16,56,128]{2,1,0:T(8,128)S(1)} %bitcast.32), channel_id=1, replica_groups={{0,2,4,6,8,10,12,14,16,18,20,22,24,26,28,30},{1,3,5,7,9,11,13,15,17,19,..., dimensions={0} | all-to-all | bytes 917504 | tf_op jit(solution)/shard_map/all_to_all | solution.py:786
  177.5 3.4 %field_part.5 = (f32[1536,128]{1,0:T(8,128)S(1)}, f32[1536,128]{1,0:T(8,128)S(1)}, f32[1024,128]{1,0:T(8,128)S(1)}) custom-call(bf16[256,128]{1,0:T(8,128)(2,1)S(1)} %get-tuple-element.237.after_ref.values_ref, f32[1536,128]{1,0:T(8,128)S(1)} %get-tuple-element.240.local_ref, f32[1536,128]{1,0:T(8,128)S(1)} %get-tuple-element.176.weight_ref, ...), custom_call_target="tpu_custom_call" | custom-call | bytes 9000000 | tf_op jit(solution)/shard_map/field_part/pallas_call | solution.py:48
  191.3 3.1 %collective-permute-done.29.a1 = f32[256,128]{1,0:T(8,128)S(1)} collective-permute-done((f32[256,128]{1,0:T(8,128)S(1)}, f32[256,128]{1,0:T(8,128)S(1)}, u32[]{:S(2)}, u32[]{:S(2)}) %collective-permute-start.29) | collective-permute-done | bytes 131104 | tf_op jit(solution)/shard_map/ppermute | solution.py:682
  194.4 11.0 %all_to_all.69 = f32[32,8,128]{2,1,0:T(8,128)S(1)} all-to-all(f32[32,8,128]{2,1,0:T(8,128)S(1)} %bitcast.36), channel_id=1, replica_groups=mesh['sub'=32] {'sub'}, dimensions={0} | all-to-all | bytes 262144 | tf_op jit(solution)/shard_map/all_to_all | solution.py:992
  (92 shorter events, 51.2 us)
Async XLA Ops:
  3.6 19.1 %collective-permute-start = (f32[256,128]{1,0:T(8,128)S(1)}, f32[256,128]{1,0:T(8,128)S(1)}, u32[]{:S(2)}, u32[]{:S(2)}) collective-permute-start(f32[256,128]{1,0:T(8,128)S(1)} %get-tuple-element.141), channel_id=1, source_target_pairs={{0,24},{1,25},{2,26},{3,27},{4,28},{5,29},{6,30},{7,31},{8,16},{9,... | collective-permute-start | bytes 393224 | tf_op jit(solution)/shard_map/ppermute | solution.py:682
  8.7 14.0 %collective-permute-start.1 = (f32[256,128]{1,0:T(8,128)S(1)}, f32[256,128]{1,0:T(8,128)S(1)}, u32[]{:S(2)}, u32[]{:S(2)}) collective-permute-start(f32[256,128]{1,0:T(8,128)S(1)} %get-tuple-element.142), channel_id=1, source_target_pairs={{0,31},{1,2},{2,1},{3,4},{4,3},{5,6},{6,5},{7,8},{8,7},{9,10},{10,... | collective-permute-start | bytes 393224 | tf_op jit(solution)/shard_map/ppermute | solution.py:682
  10.1 12.6 %collective-permute-start.2 = (f32[256,128]{1,0:T(8,128)S(1)}, f32[256,128]{1,0:T(8,128)S(1)}, u32[]{:S(2)}, u32[]{:S(2)}) collective-permute-start(f32[256,128]{1,0:T(8,128)S(1)} %get-tuple-element.143), channel_id=1, source_target_pairs={{0,8},{1,9},{2,10},{3,11},{4,12},{5,13},{6,14},{7,15},{8,0},{9,1},... | collective-permute-start | bytes 393224 | tf_op jit(solution)/shard_map/ppermute | solution.py:682
  11.8 11.0 %collective-permute-start.3 = (f32[256,128]{1,0:T(8,128)S(1)}, f32[256,128]{1,0:T(8,128)S(1)}, u32[]{:S(2)}, u32[]{:S(2)}) collective-permute-start(f32[256,128]{1,0:T(8,128)S(1)} %get-tuple-element.144), channel_id=1, source_target_pairs={{0,1},{1,0},{2,3},{3,2},{4,5},{5,4},{6,7},{7,6},{8,9},{9,8},{10,11... | collective-permute-start | bytes 393224 | tf_op jit(solution)/shard_map/ppermute | solution.py:682
  27.7 24.2 %all-to-all-start.2 = ((f32[32,48,128]{2,1,0:T(8,128)}), f32[32,48,128]{2,1,0:T(8,128)S(1)}, u32[]{:S(2)}, u32[]{:S(2)}) async-start(f32[32,48,128]{2,1,0:T(8,128)} %bitcast.10), calls=%async_computation.2 | async-start | bytes 1572864 | tf_op jit(solution)/shard_map/all_to_all | solution.py:725
  52.0 21.0 %all-to-all-start.1 = ((f32[16,56,128]{2,1,0:T(8,128)}), f32[16,56,128]{2,1,0:T(8,128)S(1)}, u32[]{:S(2)}, u32[]{:S(2)}) async-start(f32[16,56,128]{2,1,0:T(8,128)} %bitcast.7), calls=%async_computation.1 | async-start | bytes 917504 | tf_op jit(solution)/shard_map/all_to_all | solution.py:786
  61.8 11.2 %collective-permute-start.4 = (f32[48,768]{1,0:T(8,128)S(1)}, f32[48,768]{1,0:T(8,128)S(1)}, u32[]{:S(2)}, u32[]{:S(2)}) collective-permute-start(f32[48,768]{1,0:T(8,128)S(1)} %get-tuple-element.159), channel_id=1, source_target_pairs={{0,1},{1,0},{2,3},{3,2},{4,5},{5,4},{6,7},{7,6},{8,9},{9,8},{10,11... | collective-permute-start | bytes 442376 | tf_op jit(solution)/shard_map/ppermute | solution.py:783
  76.4 13.7 %collective-permute-start.6 = (f32[256,128]{1,0:T(8,128)S(1)}, f32[256,128]{1,0:T(8,128)S(1)}, u32[]{:S(2)}, u32[]{:S(2)}) collective-permute-start(f32[256,128]{1,0:T(8,128)S(1)} %get-tuple-element.167), channel_id=1, source_target_pairs={{0,24},{1,25},{2,26},{3,27},{4,28},{5,29},{6,30},{7,31},{8,16},{9,... | collective-permute-start | bytes 393224 | tf_op jit(solution)/shard_map/ppermute | solution.py:682
  79.4 10.8 %collective-permute-start.7 = (f32[256,128]{1,0:T(8,128)S(1)}, f32[256,128]{1,0:T(8,128)S(1)}, u32[]{:S(2)}, u32[]{:S(2)}) collective-permute-start(f32[256,128]{1,0:T(8,128)S(1)} %get-tuple-element.168), channel_id=1, source_target_pairs={{0,31},{1,2},{2,1},{3,4},{4,3},{5,6},{6,5},{7,8},{8,7},{9,10},{10,... | collective-permute-start | bytes 393224 | tf_op jit(solution)/shard_map/ppermute | solution.py:682
  81.1 9.0 %collective-permute-start.8 = (f32[256,128]{1,0:T(8,128)S(1)}, f32[256,128]{1,0:T(8,128)S(1)}, u32[]{:S(2)}, u32[]{:S(2)}) collective-permute-start(f32[256,128]{1,0:T(8,128)S(1)} %get-tuple-element.169), channel_id=1, source_target_pairs={{0,8},{1,9},{2,10},{3,11},{4,12},{5,13},{6,14},{7,15},{8,0},{9,1},... | collective-permute-start | bytes 393224 | tf_op jit(solution)/shard_map/ppermute | solution.py:682
  90.9 11.3 %collective-permute-start.10 = (f32[256,128]{1,0:T(8,128)S(1)}, f32[256,128]{1,0:T(8,128)S(1)}, u32[]{:S(2)}, u32[]{:S(2)}) collective-permute-start(f32[256,128]{1,0:T(8,128)S(1)} %get-tuple-element.182), channel_id=1, source_target_pairs={{0,24},{1,25},{2,26},{3,27},{4,28},{5,29},{6,30},{7,31},{8,16},{9,... | collective-permute-start | bytes 393224 | tf_op jit(solution)/shard_map/ppermute | solution.py:682
  91.8 10.4 %collective-permute-start.11 = (f32[256,128]{1,0:T(8,128)S(1)}, f32[256,128]{1,0:T(8,128)S(1)}, u32[]{:S(2)}, u32[]{:S(2)}) collective-permute-start(f32[256,128]{1,0:T(8,128)S(1)} %get-tuple-element.183), channel_id=1, source_target_pairs={{0,31},{1,2},{2,1},{3,4},{4,3},{5,6},{6,5},{7,8},{8,7},{9,10},{10,... | collective-permute-start | bytes 393224 | tf_op jit(solution)/shard_map/ppermute | solution.py:682
  93.5 8.7 %collective-permute-start.12 = (f32[256,128]{1,0:T(8,128)S(1)}, f32[256,128]{1,0:T(8,128)S(1)}, u32[]{:S(2)}, u32[]{:S(2)}) collective-permute-start(f32[256,128]{1,0:T(8,128)S(1)} %get-tuple-element.184), channel_id=1, source_target_pairs={{0,8},{1,9},{2,10},{3,11},{4,12},{5,13},{6,14},{7,15},{8,0},{9,1},... | collective-permute-start | bytes 393224 | tf_op jit(solution)/shard_map/ppermute | solution.py:682
  123.7 14.9 %collective-permute-start.15 = (f32[256,128]{1,0:T(8,128)S(1)}, f32[256,128]{1,0:T(8,128)S(1)}, u32[]{:S(2)}, u32[]{:S(2)}) collective-permute-start(f32[256,128]{1,0:T(8,128)S(1)} %get-tuple-element.207), channel_id=1, source_target_pairs={{0,24},{1,25},{2,26},{3,27},{4,28},{5,29},{6,30},{7,31},{8,16},{9,... | collective-permute-start | bytes 393224 | tf_op jit(solution)/shard_map/ppermute | solution.py:682
  125.4 13.2 %collective-permute-start.16 = (f32[256,128]{1,0:T(8,128)S(1)}, f32[256,128]{1,0:T(8,128)S(1)}, u32[]{:S(2)}, u32[]{:S(2)}) collective-permute-start(f32[256,128]{1,0:T(8,128)S(1)} %get-tuple-element.208), channel_id=1, source_target_pairs={{0,31},{1,2},{2,1},{3,4},{4,3},{5,6},{6,5},{7,8},{8,7},{9,10},{10,... | collective-permute-start | bytes 393224 | tf_op jit(solution)/shard_map/ppermute | solution.py:682
  127.8 10.9 %collective-permute-start.17 = (f32[256,128]{1,0:T(8,128)S(1)}, f32[256,128]{1,0:T(8,128)S(1)}, u32[]{:S(2)}, u32[]{:S(2)}) collective-permute-start(f32[256,128]{1,0:T(8,128)S(1)} %get-tuple-element.209), channel_id=1, source_target_pairs={{0,8},{1,9},{2,10},{3,11},{4,12},{5,13},{6,14},{7,15},{8,0},{9,1},... | collective-permute-start | bytes 393224 | tf_op jit(solution)/shard_map/ppermute | solution.py:682
  128.0 10.6 %collective-permute-start.18 = (f32[256,128]{1,0:T(8,128)S(1)}, f32[256,128]{1,0:T(8,128)S(1)}, u32[]{:S(2)}, u32[]{:S(2)}) collective-permute-start(f32[256,128]{1,0:T(8,128)S(1)} %get-tuple-element.210), channel_id=1, source_target_pairs={{0,1},{1,0},{2,3},{3,2},{4,5},{5,4},{6,7},{7,6},{8,9},{9,8},{10,11... | collective-permute-start | bytes 393224 | tf_op jit(solution)/shard_map/ppermute | solution.py:682
  139.4 11.6 %collective-permute-start.19 = (f32[256,128]{1,0:T(8,128)S(1)}, f32[256,128]{1,0:T(8,128)S(1)}, u32[]{:S(2)}, u32[]{:S(2)}) collective-permute-start(f32[256,128]{1,0:T(8,128)S(1)} %get-tuple-element.216), channel_id=1, source_target_pairs={{0,24},{1,25},{2,26},{3,27},{4,28},{5,29},{6,30},{7,31},{8,16},{9,... | collective-permute-start | bytes 393224 | tf_op jit(solution)/shard_map/ppermute | solution.py:682
  139.8 11.2 %collective-permute-start.20 = (f32[256,128]{1,0:T(8,128)S(1)}, f32[256,128]{1,0:T(8,128)S(1)}, u32[]{:S(2)}, u32[]{:S(2)}) collective-permute-start(f32[256,128]{1,0:T(8,128)S(1)} %get-tuple-element.217), channel_id=1, source_target_pairs={{0,31},{1,2},{2,1},{3,4},{4,3},{5,6},{6,5},{7,8},{8,7},{9,10},{10,... | collective-permute-start | bytes 393224 | tf_op jit(solution)/shard_map/ppermute | solution.py:682
  143.2 8.0 %collective-permute-start.21 = (f32[256,128]{1,0:T(8,128)S(1)}, f32[256,128]{1,0:T(8,128)S(1)}, u32[]{:S(2)}, u32[]{:S(2)}) collective-permute-start(f32[256,128]{1,0:T(8,128)S(1)} %get-tuple-element.218), channel_id=1, source_target_pairs={{0,8},{1,9},{2,10},{3,11},{4,12},{5,13},{6,14},{7,15},{8,0},{9,1},... | collective-permute-start | bytes 393224 | tf_op jit(solution)/shard_map/ppermute | solution.py:682
  171.3 9.6 %collective-permute-start.24 = (f32[256,128]{1,0:T(8,128)S(1)}, f32[256,128]{1,0:T(8,128)S(1)}, u32[]{:S(2)}, u32[]{:S(2)}) collective-permute-start(f32[256,128]{1,0:T(8,128)S(1)} %get-tuple-element.243), channel_id=1, source_target_pairs={{0,24},{1,25},{2,26},{3,27},{4,28},{5,29},{6,30},{7,31},{8,16},{9,... | collective-permute-start | bytes 393224 | tf_op jit(solution)/shard_map/ppermute | solution.py:682
  173.0 9.0 %collective-permute-start.25 = (f32[256,128]{1,0:T(8,128)S(1)}, f32[256,128]{1,0:T(8,128)S(1)}, u32[]{:S(2)}, u32[]{:S(2)}) collective-permute-start(f32[256,128]{1,0:T(8,128)S(1)} %get-tuple-element.244), channel_id=1, source_target_pairs={{0,31},{1,2},{2,1},{3,4},{4,3},{5,6},{6,5},{7,8},{8,7},{9,10},{10,... | collective-permute-start | bytes 393224 | tf_op jit(solution)/shard_map/ppermute | solution.py:682
  175.0 8.1 %collective-permute-start.26 = (f32[256,128]{1,0:T(8,128)S(1)}, f32[256,128]{1,0:T(8,128)S(1)}, u32[]{:S(2)}, u32[]{:S(2)}) collective-permute-start(f32[256,128]{1,0:T(8,128)S(1)} %get-tuple-element.245), channel_id=1, source_target_pairs={{0,8},{1,9},{2,10},{3,11},{4,12},{5,13},{6,14},{7,15},{8,0},{9,1},... | collective-permute-start | bytes 393224 | tf_op jit(solution)/shard_map/ppermute | solution.py:682
  185.5 8.9 %collective-permute-start.29 = (f32[256,128]{1,0:T(8,128)S(1)}, f32[256,128]{1,0:T(8,128)S(1)}, u32[]{:S(2)}, u32[]{:S(2)}) collective-permute-start(f32[256,128]{1,0:T(8,128)S(1)} %get-tuple-element.259), channel_id=1, source_target_pairs={{0,31},{1,2},{2,1},{3,4},{4,3},{5,6},{6,5},{7,8},{8,7},{9,10},{10,... | collective-permute-start | bytes 393224 | tf_op jit(solution)/shard_map/ppermute | solution.py:682
  (14 other events, 133.9 us)
where the time goes:
time: 208 us
  Pallas kernels  93.6 us (45%)
  blocking collectives  58.1 us (28%)
  starting transfers between devices  44.7 us (21%)
  waiting for transfers between devices  8.47 us (4%)
    pallas_call x34, Pallas kernels, call(): pl.pallas_call(kernel, name=name, out_shape=tuple(outs), in_specs=[specs....  93.6 us
    all_to_all x2, blocking collectives, share(): lax.all_to_all(send, 'sub', 0, 0, tiled=True, axis_index_groups=cores)  36.8 us
    ppermute x28, starting transfers between devices, exchange(): return [lax.ppermute(out, 'sub', swap) for out, swap in zip(outs, swaps)]  34.8 us
    all_to_all x1, blocking collectives, body(): sums = lax.all_to_all(send, 'sub', 0, 0, tiled=True)  11 us
    all_to_all x1, blocking collectives, body(): maps = lax.all_to_all(maps, 'sub', 0, 0, tiled=True)  10.3 us
    all_to_all x1, starting transfers between devices, share(): lax.all_to_all(send, 'sub', 0, 0, tiled=True, axis_index_groups=cores)  6.87 us
    ppermute x28, waiting for transfers between devices, exchange(): return [lax.ppermute(out, 'sub', swap) for out, swap in zip(outs, swaps)]  6.7 us
  transfers between devices with their start and end apart: 34, of which 8 were waited for; matrix products, arithmetic and copies ran while one was open for 0% of the time, Pallas kernels for 38%

commit v1 on v0

--- a/solution.py
+++ b/solution.py
@@ -167,8 +167,15 @@
     basis2_ref[ncl:, :] = low
 
 
-def loads_kernel(rows_ref, loads_from, listed_ref, out0, out1, out2, out3, pick, cat, loads, sems):
-    copies = bring([(loads_from, loads)], sems)
+def loads_kernel(rows_from, loads_from, map_from, listed_ref, maps_ref, out0, out1, out2, out3,
+                 pick, cat, loads, rows_ref, map_ref, sems):
+    *firsts, last = bring([(rows_from, rows_ref), (map_from, map_ref), (loads_from, loads)], sems)
+    copies = [last]
+    for copy in firsts:
+        copy.wait()
+    size, ncl = maps_ref.shape[0], map_ref.shape[1]
+    maps_ref[...] = jnp.zeros_like(maps_ref)
+    maps_ref[:, :ncl] = jnp.broadcast_to(map_ref[...], (size, ncl))
     me = lax.axis_index("sub")
     one = me % 2 == 0
     far_one = (me // STRIDE) % 2 == 0
@@ -245,27 +252,13 @@
     each(rows, FINE, product)
 
 
-def shared_products_kernel(local_place_ref, after_ref, pick_ref, weight_ref, local_shared_ref):
-    slots = pick_ref.shape[0]
-    weight = weight_ref[...].astype(BF16)
-
-    def some(lo):
-        at = pl.ds(lo, FINE)
-        shared = dot(pick_ref[at, :], local_place_ref[...])
-        turned = dot(pick_ref[at, :], weight)
-        for left in range(0, slots, LANES):
-            scaled = shared[:, left : left + LANES] * turned
-            local_shared_ref[at, left : left + LANES] = scaled.astype(BF16)
-
-    each(slots, FINE, some)
-
-
 def tables_kernel(row_ref, count_ref, basis_ref, after_ref, stiff_from, stiff_place_from,
-                  stiff_shared_from,
+                  stiff_shared_from, local_from,
                   pick_ref, place_ref, weight_ref, basis2_ref, basis3_ref,
-                  stiff_ref, stiff_place_ref, stiff_shared_ref, sems):
+                  stiff_ref, stiff_place_ref, stiff_shared_ref, local_ref, sems):
     copies = bring(
         [
+            (local_from, local_ref),
             (stiff_from, stiff_ref),
             (stiff_shared_from, stiff_shared_ref),
             (stiff_place_from, stiff_place_ref),
@@ -281,8 +274,10 @@
         copy.wait()
 
 
-def small_kernel(after_ref, first_from, second_from, first_ref, second_ref, sems):
-    for copy in bring([(first_from, first_ref), (second_from, second_ref)], sems):
+def small_kernel(after_ref, *refs):
+    *refs, sems = refs
+    number = len(refs) // 2
+    for copy in bring(list(zip(refs[:number], refs[number:])), sems):
         copy.wait()
 
 
@@ -349,19 +344,21 @@
         send_ref[g * rows : (g + 1) * rows, :] = block
 
 
-def front(inverse_ref, weight_ref, pick_ref, cat, local_ref, out_ref, cat2):
+def front(inverse_ref, weight_ref, pick_ref, cat, local_ref, out_ref, cat2, flat=False):
+    large, small = (FINE, FINE) if flat else (HALF, SLOTS)
+
     def product(lo):
-        at = pl.ds(lo, HALF)
+        at = pl.ds(lo, large)
         local = halves(dot(inverse_ref[at, :], cat[...]))
         local_ref[at, :] = local
         cat2[at, :] = pair(weight_ref[at, :] * local)
 
     def shared(lo):
-        at = pl.ds(lo, SLOTS)
+        at = pl.ds(lo, small)
         out_ref[at, :] = halves(dot(pick_ref[at, :], cat2[...]))
 
-    each(inverse_ref.shape[0], HALF, product)
-    each(pick_ref.shape[0], SLOTS, shared)
+    each(inverse_ref.shape[0], large, product, flat)
+    each(pick_ref.shape[0], small, shared, flat)
 
 
 def first_kernel(loads_ref, a0, a1, a2, a3, row_ref, count_ref, basis_ref, inverse_from,
@@ -546,26 +543,22 @@
     for lo, n in tiles(w_ref.shape[0], FINE):
         at = slice(lo, lo + n)
         cat[at, :] = pair(weight_ref[at, :] * w_ref[at, :])
-    front(inverse_ref, weight_ref, pick_ref, cat, local_ref, pre_ref, cat2)
-
-
-def local_shared_kernel(pre_ref, arr_ref, after_ref, local_shared_ref, scal_ref, out_ref):
-    factor = -scal_ref[0:1, :] / scal_ref[1:2, :]
-    for lo, n in tiles(pre_ref.shape[0]):
-        at = slice(lo, lo + n)
-        came = halves(dot(local_shared_ref[at, :], arr_ref[...]))
-        out_ref[at, :] = pre_ref[at, :] + factor * came
-
-
-def local_again_kernel(pre_ref, arr_ref, after_ref, local_place_ref, weight_ref, pick_ref,
-                       out_ref, cat):
+    front(inverse_ref, weight_ref, pick_ref, cat, local_ref, pre_ref, cat2, True)
+
+
+def local_shared_kernel(pre_ref, arr_ref, after_ref, local_place_ref, weight_ref, pick_ref,
+                        *refs):
+    *scal, out_ref, cat = refs
     for lo, n in tiles(weight_ref.shape[0], FINE):
         at = slice(lo, lo + n)
         came = halves(dot(local_place_ref[at, :], arr_ref[...]))
         cat[at, :] = pair(weight_ref[at, :] * came)
     for lo, n in tiles(pre_ref.shape[0], FINE):
         at = slice(lo, lo + n)
-        out_ref[at, :] = pre_ref[at, :] + halves(dot(pick_ref[at, :], cat[...]))
+        came = halves(dot(pick_ref[at, :], cat[...]))
+        if scal:
+            came *= -scal[0][0:1, :] / scal[0][1:2, :]
+        out_ref[at, :] = pre_ref[at, :] + came
 
 
 def complete_kernel(w_part_ref, local_part_ref, arr_ref, after_ref, place_ref, local_place_ref,
@@ -624,9 +617,8 @@
         return tuple(old + folded(new) for old, new in zip(sums, news))
 
     sums = summed(r1_ref.shape[0], TILE, some, (jnp.zeros((8, rhs), F32),) * 4)
-    block = collect(sums, rhs)
-    for g in range(send_ref.shape[0] // SCAL):
-        send_ref[g * SCAL : (g + 1) * SCAL, :] = block
+    wide = jnp.concatenate([jnp.sum(s, axis=0, keepdims=True) for s in sums], axis=1)
+    send_ref[...] = jnp.broadcast_to(wide, send_ref.shape)
     state_ref[...] = jnp.concatenate(
         [scal_ref[0:1, :], energy, alpha, jnp.zeros((SCAL - 3, rhs), F32)], axis=0
     )
@@ -636,7 +628,9 @@
                 x2, u2, p1, r2, half, s1,
                 x3_to, r3_to, arr_cat, x3, r3, out_sems):
     state = state_ref[...]
-    now = jnp.sum(got_ref[...].reshape(-1, SCAL, got_ref.shape[1]), axis=0)
+    total = jnp.sum(got_ref[...], axis=0, keepdims=True)
+    rhs = state.shape[1]
+    now = jnp.concatenate([total[:, k * rhs : (k + 1) * rhs] for k in range(4)], axis=0)
     beta, alpha, _ = step_scalars(state, now)
     old = state[2:3, :]
     arrivals((a0, a1, a2, a3), arr_cat)
@@ -694,17 +688,22 @@
     basis = coarse_basis[0]
     (loads_aside,) = aside(loads[0])
 
-    listed, *outs = call(
+    listed, maps, *outs = call(
         loads_kernel,
         "loads",
-        (shared_rows[0], loads_aside),
-        [far((1, lists), jnp.int32)] + out4,
-        [pick_like, wide, pltpu.VMEM(fields, F32), pltpu.SemaphoreType.DMA((1,))],
-        {1: ASPEC},
+        (*aside(shared_rows[0]), loads_aside, *aside(coarse_map)),
+        [far((1, lists), jnp.int32), far((size, LANES * pl.cdiv(ncl, LANES)), jnp.int32)] + out4,
+        [
+            pick_like,
+            wide,
+            pltpu.VMEM(fields, F32),
+            pltpu.VMEM((slots, cap), jnp.int32),
+            pltpu.VMEM((1, ncl), jnp.int32),
+            pltpu.SemaphoreType.DMA((3,)),
+        ],
+        {0: ASPEC, 1: ASPEC, 2: ASPEC},
     )
     arrived = exchange(outs)
-    own_map = jnp.pad(coarse_map, ((0, 0), (0, -ncl % LANES)))
-    maps = jnp.broadcast_to(own_map, (size, own_map.shape[1]))
     maps = lax.all_to_all(maps, "sub", 0, 0, tiled=True)
     maps, *arrived = lax.optimization_barrier((maps, *arrived))
 
@@ -809,7 +808,7 @@
     tables = held(*call(
         tables_kernel,
         "tables",
-        (listed, counts, basis, after, stiff, stiff_place, stiff_shared),
+        (listed, counts, basis, after, stiff, stiff_place, stiff_shared, local),
         [
             near((lists, rows), BF16),
             near((rows, lists), BF16),
@@ -819,13 +818,13 @@
             near((rows, rows), BF16),
             near((rows, lists), BF16),
             near((lists, lists), BF16),
+            near(fields),
         ],
-        [pltpu.SemaphoreType.DMA((3,))],
-        {4: ASPEC, 5: ASPEC, 6: ASPEC},
+        [pltpu.SemaphoreType.DMA((4,))],
+        {4: ASPEC, 5: ASPEC, 6: ASPEC, 7: ASPEC},
         us=5,
     ))
-    pick, place, weight, basis2, basis3, stiff, stiff_place, stiff_shared = tables
-    tables = []
+    pick, place, weight, basis2, basis3, stiff, stiff_place, stiff_shared, local = tables
     (coarse,) = held(coarse)
 
     def correct(terms, pre, bring_in=None):
@@ -854,25 +853,22 @@
         return held(*call(
             small_kernel,
             "small_tables",
-            (own, pick_basis, basis_place),
-            [near(pick_basis.shape, BF16), near(basis_place.shape, BF16)],
-            [pltpu.SemaphoreType.DMA((2,))],
-            {1: ASPEC, 2: ASPEC},
+            (own, pick_basis, basis_place, pre),
+            [near(pick_basis.shape, BF16), near(basis_place.shape, BF16), near(pre.shape)],
+            [pltpu.SemaphoreType.DMA((3,))],
+            {1: ASPEC, 2: ASPEC, 3: ASPEC},
             us=1,
         ))
 
-    def operate(values, local, arrived, *beside):
+    def operate(values, local, arrived, flat=False):
         part, image, pre = held(*call(
-            functools.partial(part_kernel, not tables),
+            functools.partial(part_kernel, flat),
             "field_part",
             (values, local, weight, basis3, stiff, pick),
             [near(fields), near(fields), near((lists, rhs))],
             [wide, wide],
             us=3,
         ))
-        if beside:
-            pre, table = held(*lax.optimization_barrier((pre, *beside)))
-            tables.append(table)
         arr, *outs = call(
             shared_kernel,
             "image_shared",
@@ -902,24 +898,12 @@
             us=3,
         ))
 
-    def local_shared(pre, arr, scal):
+    def local_shared(pre, arr, *scal):
         def of(own):
             return held(*call(
                 local_shared_kernel,
                 "local_shared",
-                (pre, arr, own, shared_table, scal),
-                [near((lists, rhs))],
-                us=1,
-            ))[0]
-
-        return of
-
-    def local_again(pre, arr):
-        def of(own):
-            return held(*call(
-                local_again_kernel,
-                "local_again",
-                (pre, arr, own, local_place, weight, pick),
+                (pre, arr, own, local_place, weight, pick, *scal),
                 [near((lists, rhs))],
                 [wide],
                 us=1,
@@ -936,9 +920,8 @@
             us=2,
         ))
 
-    values, _, arrived = correct(terms, lambda own: pre, bring_small)
-    part, image, arr, arrived = operate(values, local, arrived)
-    tables.append(None)
+    values, _, arrived = correct(terms, lambda own: small[2], bring_small)
+    part, image, arr, arrived = operate(values, local, arrived, True)
     u0, w0, terms, sums, inverse, local_place = held(*call(
         start_kernel,
         "start",
@@ -952,18 +935,9 @@
     local, pre = local_part(w0)
     terms, pre = held(*lax.optimization_barrier((terms, pre)))
     arr, terms = share_terms(arrived, terms, sums)
-    values, scal0, arrived = correct(terms, local_again(pre, arr))
+    values, scal0, arrived = correct(terms, local_shared(pre, arr))
     w0, local = complete(w0, local, arr, values)
-    (shared_table,) = held(*call(
-        shared_products_kernel,
-        "shared_products",
-        (local_place, values, pick, weight),
-        [near((lists, lists), BF16)],
-        us=4,
-    ))
-
-    part, image, arr, arrived = operate(values, local, arrived, shared_table)
-    shared_table = tables[-1]
+    part, image, arr, arrived = operate(values, local, arrived)
     m0, z0, x1, r1, u1, w1, terms, sums = held(*call(
         second_kernel,
         "first_update",
@@ -984,7 +958,7 @@
         "second_update",
         (part, image, arr, scal0, scal1, x1, r1, u1, w1, u0, w0, m0, z0)
         + (place, stiff_place, weight),
-        [far((size * SCAL, rhs)), far((SCAL, rhs))] + [near(fields)] * 6,
+        [far((size, 4 * rhs)), far((SCAL, rhs))] + [near(fields)] * 6,
         us=4,
     )
     x2, r2, u2, half, p1, s1 = held(*news)

time: 208 us -> 202 us (0.971)
  Pallas kernels: 93.6 us -> 87.2 us
  waiting for transfers between devices: 8.47 us -> 11.1 us
    pallas_call x34 -> x33, Pallas kernels: 93.6 us -> 87.2 us  [call(): pl.pallas_call(kernel, name=name, out_shape=tuple(outs), in_specs=[specs....]
    ppermute x28, waiting for transfers between devices: 6.7 us -> 9.9 us  [exchange(): return [lax.ppermute(out, 'sub', swap) for out, swap in zip(outs, swaps)]]
  transfers between devices with their start and end apart: 34 -> 34, of which waited for: 8 -> 9; matrix products, arithmetic and copies ran while one was open for 0% -> 0% of each run, Pallas kernels for 38% -> 36%
where the time goes in v1:
time: 202 us; the launch traced here: 201 us
  Pallas kernels  87.2 us (43%)
  blocking collectives  57.2 us (28%)
  starting transfers between devices  44.5 us (22%)
  waiting for transfers between devices  11.1 us (5%)
    pallas_call x33, Pallas kernels, call(): pl.pallas_call(kernel, name=name, out_shape=tuple(outs), in_specs=[specs....  87.2 us
    all_to_all x2, blocking collectives, share(): lax.all_to_all(send, 'sub', 0, 0, tiled=True, axis_index_groups=cores)  36.8 us
    ppermute x28, starting transfers between devices, exchange(): return [lax.ppermute(out, 'sub', swap) for out, swap in zip(outs, swaps)]  34.5 us
    all_to_all x1, blocking collectives, body(): maps = lax.all_to_all(maps, 'sub', 0, 0, tiled=True)  10.3 us
    all_to_all x1, blocking collectives, body(): sums = lax.all_to_all(send, 'sub', 0, 0, tiled=True)  10.1 us
    ppermute x28, waiting for transfers between devices, exchange(): return [lax.ppermute(out, 'sub', swap) for out, swap in zip(outs, swaps)]  9.9 us
    all_to_all x1, starting transfers between devices, share(): lax.all_to_all(send, 'sub', 0, 0, tiled=True, axis_index_groups=cores)  6.87 us
  transfers between devices with their start and end apart: 34, of which 9 were waited for; matrix products, arithmetic and copies ran while one was open for 0% of the time, Pallas kernels for 36%

profile of v1, /device:TPU:0, one launch (start us, length us, event | category | flops | bytes accessed | tf_op | source)
XLA Modules:
  0.0 201.5 jit_solution(15153928771047520933)
XLA Ops:
  0.7 3.0 %loads.1 = (s32[1,1024]{1,0:T(1,128)S(1)}, s32[32,128]{1,0:T(8,128)S(1)}, f32[256,128]{1,0:T(8,128)S(1)}, f32[256,128]{1,0:T(8,128)S(1)}, f32[256,128]{1,0:T(8,128)S(1)}, /*index=5*/f32[256,128]{1,0:T(8,128)S(1)}) custom-call(s32[4,256]{1,0:T(4,128)} %bitcast.46, f32[1536,128]{1,0:T(8,128)} %bitcast.27, s32[1,48]{1,0:T(1,128)} %map_from.1), custom_call_target="tpu_custom_call" | custom-call | bytes 6000000 | tf_op jit(solution)/shard_map/loads/pallas_call | solution.py:48
  3.6 5.1 %collective-permute-start = (f32[256,128]{1,0:T(8,128)S(1)}, f32[256,128]{1,0:T(8,128)S(1)}, u32[]{:S(2)}, u32[]{:S(2)}) collective-permute-start(f32[256,128]{1,0:T(8,128)S(1)} %get-tuple-element.143), channel_id=1, source_target_pairs={{0,24},{1,25},{2,26},{3,27},{4,28},{5,29},{6,30},{7,31},{8,16},{9,... | collective-permute-start | bytes 393224 | tf_op jit(solution)/shard_map/ppermute | solution.py:676
  11.8 10.3 %all_to_all.69 = s32[32,1,128]{2,1,0:T(1,128)S(1)} all-to-all(s32[32,1,128]{2,1,0:T(1,128)S(1)} %bitcast.40), channel_id=1, replica_groups=mesh['sub'=32] {'sub'}, dimensions={0} | all-to-all | bytes 32768 | tf_op jit(solution)/shard_map/all_to_all | solution.py:707
  22.1 4.9 %coarse_columns.1 = f32[1536,128]{1,0:T(8,128)} custom-call(s32[32,128]{1,0:T(8,128)S(1)} %bitcast.37, f32[128,4096]{1,0:T(8,128)} %inverse_from.1), custom_call_target="tpu_custom_call" | custom-call | bytes 6000000 | tf_op jit(solution)/shard_map/coarse_columns/pallas_call | solution.py:48
  27.1 2.8 %all-to-all-start.2 = ((f32[32,48,128]{2,1,0:T(8,128)}), f32[32,48,128]{2,1,0:T(8,128)S(1)}, u32[]{:S(2)}, u32[]{:S(2)}) async-start(f32[32,48,128]{2,1,0:T(8,128)} %bitcast.11), calls=%async_computation.2 | async-start | bytes 1572864 | tf_op jit(solution)/shard_map/all_to_all | solution.py:724
  29.9 14.8 %products.1 = (bf16[1536,1024]{1,0:T(8,128)(2,1)}, bf16[1024,1024]{1,0:T(8,128)(2,1)}, bf16[96,1024]{1,0:T(8,128)(2,1)}, bf16[1024,256]{1,0:T(8,128)(2,1)}) custom-call(s32[1,1024]{1,0:T(1,128)S(1)} %get-tuple-element.151.row_ref, s32[1,1536]{1,0:T(1,128)S(1)} %copy-done.2, f32[48,1536]{1,0:T(8,128)S(1)} %bitcast.29, bf16[1536,1536]{1,0:T(8,128)(2,1)} %bitcast.44), custom_call_target="tpu_custom_call" | custom-call | bytes 30000000 | tf_op jit(solution)/shard_map/products/pallas_call | solution.py:48
  44.6 6.7 %residual_and_terms.1 = (f32[1536,128]{1,0:T(8,128)}, f32[1536,128]{1,0:T(8,128)}, f32[1024,128]{1,0:T(8,128)}, f32[896,128]{1,0:T(8,128)}) custom-call(f32[1536,128]{1,0:T(8,128)S(1)} %bitcast.28, f32[256,128]{1,0:T(8,128)S(1)} %collective-permute-done.a0, f32[256,128]{1,0:T(8,128)S(1)} %collective-permute-done.1.a1, ...), custom_call_target="tpu_custom_call" | custom-call | bytes 18000000 | tf_op jit(solution)/shard_map/residual_and_terms/pallas_call | solution.py:48
  51.3 6.9 %all-to-all-start.1 = ((f32[16,56,128]{2,1,0:T(8,128)}), f32[16,56,128]{2,1,0:T(8,128)S(1)}, u32[]{:S(2)}, u32[]{:S(2)}) async-start(f32[16,56,128]{2,1,0:T(8,128)} %bitcast.8), calls=%async_computation.1 | async-start | bytes 917504 | tf_op jit(solution)/shard_map/all_to_all | solution.py:785
  58.2 2.9 %coarse_block.1 = (f32[48,768]{1,0:T(8,128)S(1)}, f32[48,768]{1,0:T(8,128)S(1)}) custom-call(s32[32,128]{1,0:T(8,128)S(1)} %bitcast.38, s32[1]{0:T(128)} %bitcast.10.which_ref, f32[1536,128]{1,0:T(8,128)S(1)} %bitcast.26), custom_call_target="tpu_custom_call" | custom-call | bytes 6000000 | tf_op jit(solution)/shard_map/coarse_block/pallas_call | solution.py:48
  61.2 9.9 %local_products.1.local_place_from = bf16[1536,1024]{1,0:T(8,128)(2,1)} custom-call(s32[1,1024]{1,0:T(1,128)S(1)} %get-tuple-element.151.row_ref, s32[1,1536]{1,0:T(1,128)S(1)} %copy-done.2, f32[896,128]{1,0:T(8,128)} %get-tuple-element.157.after_ref, bf16[1536,1536]{1,0:T(8,128)(2,1)} %bitcast.42), custom_call_target="tpu_custom_call" | custom-call | bytes 30000000 | tf_op jit(solution)/shard_map/local_products/pallas_call | solution.py:48
  74.9 3.0 %collective-permute-start.6 = (f32[256,128]{1,0:T(8,128)S(1)}, f32[256,128]{1,0:T(8,128)S(1)}, u32[]{:S(2)}, u32[]{:S(2)}) collective-permute-start(f32[256,128]{1,0:T(8,128)S(1)} %get-tuple-element.170), channel_id=1, source_target_pairs={{0,24},{1,25},{2,26},{3,27},{4,28},{5,29},{6,30},{7,31},{8,16},{9,... | collective-permute-start | bytes 393224 | tf_op jit(solution)/shard_map/ppermute | solution.py:676
  81.0 4.2 %tables.1 = (bf16[1024,1536]{1,0:T(8,128)(2,1)S(1)}, bf16[1536,1024]{1,0:T(8,128)(2,1)S(1)}, f32[1536,128]{1,0:T(8,128)S(1)}, bf16[96,1536]{1,0:T(8,128)(2,1)S(1...) custom-call(s32[1,1024]{1,0:T(1,128)S(1)} %get-tuple-element.151.row, ...), custom_call_target="tpu_custom_call" | custom-call | bytes 15000000 | tf_op jit(solution)/shard_map/tables/pallas_call | solution.py:48
  85.2 2.4 %field_part.3 = (f32[1536,128]{1,0:T(8,128)S(1)}, f32[1536,128]{1,0:T(8,128)S(1)}, f32[1024,128]{1,0:T(8,128)S(1)}) custom-call(bf16[256,128]{1,0:T(8,128)(2,1)S(1)} %get-tuple-element.174.values_ref, f32[1536,128]{1,0:T(8,128)S(1)} %get-tuple-element.179.local_ref, f32[1536,128]{1,0:T(8,128)S(1)} %get-tuple-element.180.weight_ref, ...), custom_call_target="tpu_custom_call" | custom-call | bytes 9000000 | tf_op jit(solution)/shard_map/field_part/pallas_call | solution.py:48
  92.5 4.5 %start.1 = (f32[1536,128]{1,0:T(8,128)S(1)}, f32[1536,128]{1,0:T(8,128)S(1)}, f32[48,128]{1,0:T(8,128)S(1)}, f32[8,128]{1,0:T(8,128)S(1)}, bf16[1536,1536]{1,0:T...) custom-call(f32[1536,128]{1,0:T(8,128)S(1)} %get-tuple-element.190.part_ref, f32[1536,128]{1,0:T(8,128)S(1)} %get-tuple-element.191.image_ref, ...), custom_call_target="tpu_custom_call" | custom-call | bytes 9000000 | tf_op jit(solution)/shard_map/start/pallas_call | solution.py:48
  100.2 18.2 %all_to_all.70 = f32[16,56,128]{2,1,0:T(8,128)S(1)} all-to-all(f32[16,56,128]{2,1,0:T(8,128)S(1)} %bitcast.35), channel_id=1, replica_groups={{0,2,4,6,8,10,12,14,16,18,20,22,24,26,28,30},{1,3,5,7,9,11,13,15,17,19,..., dimensions={0} | all-to-all | bytes 917504 | tf_op jit(solution)/shard_map/all_to_all | solution.py:785
  122.5 2.4 %collective-permute-start.16 = (f32[256,128]{1,0:T(8,128)S(1)}, f32[256,128]{1,0:T(8,128)S(1)}, u32[]{:S(2)}, u32[]{:S(2)}) collective-permute-start(f32[256,128]{1,0:T(8,128)S(1)} %get-tuple-element.212), channel_id=1, source_target_pairs={{0,31},{1,2},{2,1},{3,4},{4,3},{5,6},{6,5},{7,8},{8,7},{9,10},{10,... | collective-permute-start | bytes 393224 | tf_op jit(solution)/shard_map/ppermute | solution.py:676
  127.3 3.4 %field_part.4 = (f32[1536,128]{1,0:T(8,128)S(1)}, f32[1536,128]{1,0:T(8,128)S(1)}, f32[1024,128]{1,0:T(8,128)S(1)}) custom-call(bf16[256,128]{1,0:T(8,128)(2,1)S(1)} %get-tuple-element.215.after_ref.values_ref, f32[1536,128]{1,0:T(8,128)S(1)} %get-tuple-element.217.local_ref, f32[1536,128]{1,0:T(8,128)S(1)} %get-tuple-element.180.weight_ref, ...), custom_call_target="tpu_custom_call" | custom-call | bytes 9000000 | tf_op jit(solution)/shard_map/field_part/pallas_call | solution.py:48
  137.3 4.0 %first_update.1 = (f32[1536,128]{1,0:T(8,128)S(1)}, f32[1536,128]{1,0:T(8,128)S(1)}, f32[1536,128]{1,0:T(8,128)S(1)}, f32[1536,128]{1,0:T(8,128)S(1)}, f32[1536,...) custom-call(f32[1536,128]{1,0:T(8,128)S(1)} %get-tuple-element.223.part_ref, ...), custom_call_target="tpu_custom_call" | custom-call | bytes 12000000 | tf_op jit(solution)/shard_map/first_update/pallas_call | solution.py:48
  144.5 18.7 %all_to_all.71 = f32[16,56,128]{2,1,0:T(8,128)S(1)} all-to-all(f32[16,56,128]{2,1,0:T(8,128)S(1)} %bitcast.34), channel_id=1, replica_groups={{0,2,4,6,8,10,12,14,16,18,20,22,24,26,28,30},{1,3,5,7,9,11,13,15,17,19,..., dimensions={0} | all-to-all | bytes 917504 | tf_op jit(solution)/shard_map/all_to_all | solution.py:785
  167.2 2.4 %collective-permute-start.25 = (f32[256,128]{1,0:T(8,128)S(1)}, f32[256,128]{1,0:T(8,128)S(1)}, u32[]{:S(2)}, u32[]{:S(2)}) collective-permute-start(f32[256,128]{1,0:T(8,128)S(1)} %get-tuple-element.246), channel_id=1, source_target_pairs={{0,31},{1,2},{2,1},{3,4},{4,3},{5,6},{6,5},{7,8},{8,7},{9,10},{10,... | collective-permute-start | bytes 393224 | tf_op jit(solution)/shard_map/ppermute | solution.py:676
  172.1 3.4 %field_part.5 = (f32[1536,128]{1,0:T(8,128)S(1)}, f32[1536,128]{1,0:T(8,128)S(1)}, f32[1024,128]{1,0:T(8,128)S(1)}) custom-call(bf16[256,128]{1,0:T(8,128)(2,1)S(1)} %get-tuple-element.239.after_ref.values_ref, f32[1536,128]{1,0:T(8,128)S(1)} %get-tuple-element.242.local_ref, f32[1536,128]{1,0:T(8,128)S(1)} %get-tuple-element.180.weight_ref, ...), custom_call_target="tpu_custom_call" | custom-call | bytes 9000000 | tf_op jit(solution)/shard_map/field_part/pallas_call | solution.py:48
  182.0 2.6 %second_update.1 = (f32[32,512]{1,0:T(8,128)S(1)}, f32[8,128]{1,0:T(8,128)S(1)}, f32[1536,128]{1,0:T(8,128)S(1)}, f32[1536,128]{1,0:T(8,128)S(1)}, f32[1536,128]...) custom-call(f32[1536,128]{1,0:T(8,128)S(1)} %get-tuple-element.243.part_ref, ...), custom_call_target="tpu_custom_call" | custom-call | bytes 12000000 | tf_op jit(solution)/shard_map/second_update/pallas_call | solution.py:48
  185.6 3.3 %collective-permute-done.29.a1 = f32[256,128]{1,0:T(8,128)S(1)} collective-permute-done((f32[256,128]{1,0:T(8,128)S(1)}, f32[256,128]{1,0:T(8,128)S(1)}, u32[]{:S(2)}, u32[]{:S(2)}) %collective-permute-start.29) | collective-permute-done | bytes 131104 | tf_op jit(solution)/shard_map/ppermute | solution.py:676
  189.0 10.1 %all_to_all.72 = f32[32,1,512]{2,1,0:T(1,128)S(1)} all-to-all(f32[32,1,512]{2,1,0:T(1,128)S(1)} %copy.11), channel_id=1, replica_groups=mesh['sub'=32] {'sub'}, dimensions={0} | all-to-all | bytes 131072 | tf_op jit(solution)/shard_map/all_to_all | solution.py:966
  (89 shorter events, 50.5 us)
Async XLA Ops:
  3.6 18.5 %collective-permute-start = (f32[256,128]{1,0:T(8,128)S(1)}, f32[256,128]{1,0:T(8,128)S(1)}, u32[]{:S(2)}, u32[]{:S(2)}) collective-permute-start(f32[256,128]{1,0:T(8,128)S(1)} %get-tuple-element.143), channel_id=1, source_target_pairs={{0,24},{1,25},{2,26},{3,27},{4,28},{5,29},{6,30},{7,31},{8,16},{9,... | collective-permute-start | bytes 393224 | tf_op jit(solution)/shard_map/ppermute | solution.py:676
  8.7 13.3 %collective-permute-start.1 = (f32[256,128]{1,0:T(8,128)S(1)}, f32[256,128]{1,0:T(8,128)S(1)}, u32[]{:S(2)}, u32[]{:S(2)}) collective-permute-start(f32[256,128]{1,0:T(8,128)S(1)} %get-tuple-element.144), channel_id=1, source_target_pairs={{0,31},{1,2},{2,1},{3,4},{4,3},{5,6},{6,5},{7,8},{8,7},{9,10},{10,... | collective-permute-start | bytes 393224 | tf_op jit(solution)/shard_map/ppermute | solution.py:676
  10.1 11.9 %collective-permute-start.2 = (f32[256,128]{1,0:T(8,128)S(1)}, f32[256,128]{1,0:T(8,128)S(1)}, u32[]{:S(2)}, u32[]{:S(2)}) collective-permute-start(f32[256,128]{1,0:T(8,128)S(1)} %get-tuple-element.145), channel_id=1, source_target_pairs={{0,8},{1,9},{2,10},{3,11},{4,12},{5,13},{6,14},{7,15},{8,0},{9,1},... | collective-permute-start | bytes 393224 | tf_op jit(solution)/shard_map/ppermute | solution.py:676
  11.8 10.3 %collective-permute-start.3 = (f32[256,128]{1,0:T(8,128)S(1)}, f32[256,128]{1,0:T(8,128)S(1)}, u32[]{:S(2)}, u32[]{:S(2)}) collective-permute-start(f32[256,128]{1,0:T(8,128)S(1)} %get-tuple-element.146), channel_id=1, source_target_pairs={{0,1},{1,0},{2,3},{3,2},{4,5},{5,4},{6,7},{7,6},{8,9},{9,8},{10,11... | collective-permute-start | bytes 393224 | tf_op jit(solution)/shard_map/ppermute | solution.py:676
  27.1 24.3 %all-to-all-start.2 = ((f32[32,48,128]{2,1,0:T(8,128)}), f32[32,48,128]{2,1,0:T(8,128)S(1)}, u32[]{:S(2)}, u32[]{:S(2)}) async-start(f32[32,48,128]{2,1,0:T(8,128)} %bitcast.11), calls=%async_computation.2 | async-start | bytes 1572864 | tf_op jit(solution)/shard_map/all_to_all | solution.py:724
  51.3 21.1 %all-to-all-start.1 = ((f32[16,56,128]{2,1,0:T(8,128)}), f32[16,56,128]{2,1,0:T(8,128)S(1)}, u32[]{:S(2)}, u32[]{:S(2)}) async-start(f32[16,56,128]{2,1,0:T(8,128)} %bitcast.8), calls=%async_computation.1 | async-start | bytes 917504 | tf_op jit(solution)/shard_map/all_to_all | solution.py:785
  61.2 11.2 %collective-permute-start.4 = (f32[48,768]{1,0:T(8,128)S(1)}, f32[48,768]{1,0:T(8,128)S(1)}, u32[]{:S(2)}, u32[]{:S(2)}) collective-permute-start(f32[48,768]{1,0:T(8,128)S(1)} %get-tuple-element.161), channel_id=1, source_target_pairs={{0,1},{1,0},{2,3},{3,2},{4,5},{5,4},{6,7},{7,6},{8,9},{9,8},{10,11... | collective-permute-start | bytes 442376 | tf_op jit(solution)/shard_map/ppermute | solution.py:782
  74.9 12.7 %collective-permute-start.6 = (f32[256,128]{1,0:T(8,128)S(1)}, f32[256,128]{1,0:T(8,128)S(1)}, u32[]{:S(2)}, u32[]{:S(2)}) collective-permute-start(f32[256,128]{1,0:T(8,128)S(1)} %get-tuple-element.170), channel_id=1, source_target_pairs={{0,24},{1,25},{2,26},{3,27},{4,28},{5,29},{6,30},{7,31},{8,16},{9,... | collective-permute-start | bytes 393224 | tf_op jit(solution)/shard_map/ppermute | solution.py:676
  77.8 9.7 %collective-permute-start.7 = (f32[256,128]{1,0:T(8,128)S(1)}, f32[256,128]{1,0:T(8,128)S(1)}, u32[]{:S(2)}, u32[]{:S(2)}) collective-permute-start(f32[256,128]{1,0:T(8,128)S(1)} %get-tuple-element.171), channel_id=1, source_target_pairs={{0,31},{1,2},{2,1},{3,4},{4,3},{5,6},{6,5},{7,8},{8,7},{9,10},{10,... | collective-permute-start | bytes 393224 | tf_op jit(solution)/shard_map/ppermute | solution.py:676
  79.5 8.1 %collective-permute-start.8 = (f32[256,128]{1,0:T(8,128)S(1)}, f32[256,128]{1,0:T(8,128)S(1)}, u32[]{:S(2)}, u32[]{:S(2)}) collective-permute-start(f32[256,128]{1,0:T(8,128)S(1)} %get-tuple-element.172), channel_id=1, source_target_pairs={{0,8},{1,9},{2,10},{3,11},{4,12},{5,13},{6,14},{7,15},{8,0},{9,1},... | collective-permute-start | bytes 393224 | tf_op jit(solution)/shard_map/ppermute | solution.py:676
  88.3 10.8 %collective-permute-start.10 = (f32[256,128]{1,0:T(8,128)S(1)}, f32[256,128]{1,0:T(8,128)S(1)}, u32[]{:S(2)}, u32[]{:S(2)}) collective-permute-start(f32[256,128]{1,0:T(8,128)S(1)} %get-tuple-element.186), channel_id=1, source_target_pairs={{0,24},{1,25},{2,26},{3,27},{4,28},{5,29},{6,30},{7,31},{8,16},{9,... | collective-permute-start | bytes 393224 | tf_op jit(solution)/shard_map/ppermute | solution.py:676
  90.2 9.0 %collective-permute-start.11 = (f32[256,128]{1,0:T(8,128)S(1)}, f32[256,128]{1,0:T(8,128)S(1)}, u32[]{:S(2)}, u32[]{:S(2)}) collective-permute-start(f32[256,128]{1,0:T(8,128)S(1)} %get-tuple-element.187), channel_id=1, source_target_pairs={{0,31},{1,2},{2,1},{3,4},{4,3},{5,6},{6,5},{7,8},{8,7},{9,10},{10,... | collective-permute-start | bytes 393224 | tf_op jit(solution)/shard_map/ppermute | solution.py:676
  91.9 8.1 %collective-permute-start.12 = (f32[256,128]{1,0:T(8,128)S(1)}, f32[256,128]{1,0:T(8,128)S(1)}, u32[]{:S(2)}, u32[]{:S(2)}) collective-permute-start(f32[256,128]{1,0:T(8,128)S(1)} %get-tuple-element.188), channel_id=1, source_target_pairs={{0,8},{1,9},{2,10},{3,11},{4,12},{5,13},{6,14},{7,15},{8,0},{9,1},... | collective-permute-start | bytes 393224 | tf_op jit(solution)/shard_map/ppermute | solution.py:676
  120.9 9.9 %collective-permute-start.15 = (f32[256,128]{1,0:T(8,128)S(1)}, f32[256,128]{1,0:T(8,128)S(1)}, u32[]{:S(2)}, u32[]{:S(2)}) collective-permute-start(f32[256,128]{1,0:T(8,128)S(1)} %get-tuple-element.211), channel_id=1, source_target_pairs={{0,24},{1,25},{2,26},{3,27},{4,28},{5,29},{6,30},{7,31},{8,16},{9,... | collective-permute-start | bytes 393224 | tf_op jit(solution)/shard_map/ppermute | solution.py:676
  122.5 9.3 %collective-permute-start.16 = (f32[256,128]{1,0:T(8,128)S(1)}, f32[256,128]{1,0:T(8,128)S(1)}, u32[]{:S(2)}, u32[]{:S(2)}) collective-permute-start(f32[256,128]{1,0:T(8,128)S(1)} %get-tuple-element.212), channel_id=1, source_target_pairs={{0,31},{1,2},{2,1},{3,4},{4,3},{5,6},{6,5},{7,8},{8,7},{9,10},{10,... | collective-permute-start | bytes 393224 | tf_op jit(solution)/shard_map/ppermute | solution.py:676
  124.9 7.9 %collective-permute-start.17 = (f32[256,128]{1,0:T(8,128)S(1)}, f32[256,128]{1,0:T(8,128)S(1)}, u32[]{:S(2)}, u32[]{:S(2)}) collective-permute-start(f32[256,128]{1,0:T(8,128)S(1)} %get-tuple-element.213), channel_id=1, source_target_pairs={{0,8},{1,9},{2,10},{3,11},{4,12},{5,13},{6,14},{7,15},{8,0},{9,1},... | collective-permute-start | bytes 393224 | tf_op jit(solution)/shard_map/ppermute | solution.py:676
  125.1 7.7 %collective-permute-start.18 = (f32[256,128]{1,0:T(8,128)S(1)}, f32[256,128]{1,0:T(8,128)S(1)}, u32[]{:S(2)}, u32[]{:S(2)}) collective-permute-start(f32[256,128]{1,0:T(8,128)S(1)} %get-tuple-element.214), channel_id=1, source_target_pairs={{0,1},{1,0},{2,3},{3,2},{4,5},{5,4},{6,7},{7,6},{8,9},{9,8},{10,11... | collective-permute-start | bytes 393224 | tf_op jit(solution)/shard_map/ppermute | solution.py:676
  133.5 10.0 %collective-permute-start.19 = (f32[256,128]{1,0:T(8,128)S(1)}, f32[256,128]{1,0:T(8,128)S(1)}, u32[]{:S(2)}, u32[]{:S(2)}) collective-permute-start(f32[256,128]{1,0:T(8,128)S(1)} %get-tuple-element.219), channel_id=1, source_target_pairs={{0,24},{1,25},{2,26},{3,27},{4,28},{5,29},{6,30},{7,31},{8,16},{9,... | collective-permute-start | bytes 393224 | tf_op jit(solution)/shard_map/ppermute | solution.py:676
  135.3 8.9 %collective-permute-start.20 = (f32[256,128]{1,0:T(8,128)S(1)}, f32[256,128]{1,0:T(8,128)S(1)}, u32[]{:S(2)}, u32[]{:S(2)}) collective-permute-start(f32[256,128]{1,0:T(8,128)S(1)} %get-tuple-element.220), channel_id=1, source_target_pairs={{0,31},{1,2},{2,1},{3,4},{4,3},{5,6},{6,5},{7,8},{8,7},{9,10},{10,... | collective-permute-start | bytes 393224 | tf_op jit(solution)/shard_map/ppermute | solution.py:676
  165.6 9.9 %collective-permute-start.24 = (f32[256,128]{1,0:T(8,128)S(1)}, f32[256,128]{1,0:T(8,128)S(1)}, u32[]{:S(2)}, u32[]{:S(2)}) collective-permute-start(f32[256,128]{1,0:T(8,128)S(1)} %get-tuple-element.245), channel_id=1, source_target_pairs={{0,24},{1,25},{2,26},{3,27},{4,28},{5,29},{6,30},{7,31},{8,16},{9,... | collective-permute-start | bytes 393224 | tf_op jit(solution)/shard_map/ppermute | solution.py:676
  167.2 9.3 %collective-permute-start.25 = (f32[256,128]{1,0:T(8,128)S(1)}, f32[256,128]{1,0:T(8,128)S(1)}, u32[]{:S(2)}, u32[]{:S(2)}) collective-permute-start(f32[256,128]{1,0:T(8,128)S(1)} %get-tuple-element.246), channel_id=1, source_target_pairs={{0,31},{1,2},{2,1},{3,4},{4,3},{5,6},{6,5},{7,8},{8,7},{9,10},{10,... | collective-permute-start | bytes 393224 | tf_op jit(solution)/shard_map/ppermute | solution.py:676
  169.6 7.9 %collective-permute-start.26 = (f32[256,128]{1,0:T(8,128)S(1)}, f32[256,128]{1,0:T(8,128)S(1)}, u32[]{:S(2)}, u32[]{:S(2)}) collective-permute-start(f32[256,128]{1,0:T(8,128)S(1)} %get-tuple-element.247), channel_id=1, source_target_pairs={{0,8},{1,9},{2,10},{3,11},{4,12},{5,13},{6,14},{7,15},{8,0},{9,1},... | collective-permute-start | bytes 393224 | tf_op jit(solution)/shard_map/ppermute | solution.py:676
  169.9 7.7 %collective-permute-start.27 = (f32[256,128]{1,0:T(8,128)S(1)}, f32[256,128]{1,0:T(8,128)S(1)}, u32[]{:S(2)}, u32[]{:S(2)}) collective-permute-start(f32[256,128]{1,0:T(8,128)S(1)} %get-tuple-element.248), channel_id=1, source_target_pairs={{0,1},{1,0},{2,3},{3,2},{4,5},{5,4},{6,7},{7,6},{8,9},{9,8},{10,11... | collective-permute-start | bytes 393224 | tf_op jit(solution)/shard_map/ppermute | solution.py:676
  180.1 8.9 %collective-permute-start.29 = (f32[256,128]{1,0:T(8,128)S(1)}, f32[256,128]{1,0:T(8,128)S(1)}, u32[]{:S(2)}, u32[]{:S(2)}) collective-permute-start(f32[256,128]{1,0:T(8,128)S(1)} %get-tuple-element.261), channel_id=1, source_target_pairs={{0,31},{1,2},{2,1},{3,4},{4,3},{5,6},{6,5},{7,8},{8,7},{9,10},{10,... | collective-permute-start | bytes 393224 | tf_op jit(solution)/shard_map/ppermute | solution.py:676
  (13 other events, 130.5 us)

commit v2 on v1

--- a/solution.py
+++ b/solution.py
@@ -15,7 +15,7 @@
 HALF = 768
 SLOTS = 512
 SCAL = 8
-ORDER = (3, 1, 2, 0)
+ORDER = (3, 0, 1, 2)
 LANES = 128
 
 VSPEC = pl.BlockSpec(memory_space=pltpu.VMEM)

time: 202 us -> 201 us (level)
  starting transfers between devices: 44.5 us -> 51.2 us
  waiting for transfers between devices: 11.1 us -> 6.28 us
  blocking collectives: 57.2 us -> 54.4 us
    ppermute x28, starting transfers between devices: 34.5 us -> 40.9 us  [exchange(): return [lax.ppermute(out, 'sub', swap) for out, swap in zip(outs, swaps)]]
    ppermute x28, waiting for transfers between devices: 9.9 us -> 5.03 us  [exchange(): return [lax.ppermute(out, 'sub', swap) for out, swap in zip(outs, swaps)]]
  transfers between devices with their start and end apart: 34 -> 34, of which waited for: 9 -> 7; matrix products, arithmetic and copies ran while one was open for 0% -> 0% of each run, Pallas kernels for 36% -> 36%
where the time goes in v2:
time: 201 us
  Pallas kernels  87.2 us (43%)
  blocking collectives  54.4 us (27%)
  starting transfers between devices  51.2 us (25%)
  waiting for transfers between devices  6.28 us (3%)
    pallas_call x33, Pallas kernels, call(): pl.pallas_call(kernel, name=name, out_shape=tuple(outs), in_specs=[specs....  87.2 us
    ppermute x28, starting transfers between devices, exchange(): return [lax.ppermute(out, 'sub', swap) for out, swap in zip(outs, swaps)]  40.9 us
    all_to_all x2, blocking collectives, share(): lax.all_to_all(send, 'sub', 0, 0, tiled=True, axis_index_groups=cores)  35.1 us
    all_to_all x1, blocking collectives, body(): sums = lax.all_to_all(send, 'sub', 0, 0, tiled=True)  10.4 us
    all_to_all x1, blocking collectives, body(): maps = lax.all_to_all(maps, 'sub', 0, 0, tiled=True)  8.92 us
    all_to_all x1, starting transfers between devices, share(): lax.all_to_all(send, 'sub', 0, 0, tiled=True, axis_index_groups=cores)  6.87 us
    ppermute x28, waiting for transfers between devices, exchange(): return [lax.ppermute(out, 'sub', swap) for out, swap in zip(outs, swaps)]  5.03 us
  transfers between devices with their start and end apart: 34, of which 7 were waited for; matrix products, arithmetic and copies ran while one was open for 0% of the time, Pallas kernels for 36%

profile of v2, /device:TPU:0, one launch (start us, length us, event | category | flops | bytes accessed | tf_op | source)
XLA Modules:
  0.0 200.5 jit_solution(8067642445530227561)
XLA Ops:
  0.7 3.0 %loads.1 = (s32[1,1024]{1,0:T(1,128)S(1)}, s32[32,128]{1,0:T(8,128)S(1)}, f32[256,128]{1,0:T(8,128)S(1)}, f32[256,128]{1,0:T(8,128)S(1)}, f32[256,128]{1,0:T(8,128)S(1)}, /*index=5*/f32[256,128]{1,0:T(8,128)S(1)}) custom-call(s32[4,256]{1,0:T(4,128)} %bitcast.46, f32[1536,128]{1,0:T(8,128)} %bitcast.27, s32[1,48]{1,0:T(1,128)} %map_from.1), custom_call_target="tpu_custom_call" | custom-call | bytes 6000000 | tf_op jit(solution)/shard_map/loads/pallas_call | solution.py:48
  3.6 5.1 %collective-permute-start = (f32[256,128]{1,0:T(8,128)S(1)}, f32[256,128]{1,0:T(8,128)S(1)}, u32[]{:S(2)}, u32[]{:S(2)}) collective-permute-start(f32[256,128]{1,0:T(8,128)S(1)} %get-tuple-element.143), channel_id=1, source_target_pairs={{0,24},{1,25},{2,26},{3,27},{4,28},{5,29},{6,30},{7,31},{8,16},{9,... | collective-permute-start | bytes 393224 | tf_op jit(solution)/shard_map/ppermute | solution.py:676
  12.8 8.9 %all_to_all.69 = s32[32,1,128]{2,1,0:T(1,128)S(1)} all-to-all(s32[32,1,128]{2,1,0:T(1,128)S(1)} %bitcast.40), channel_id=1, replica_groups=mesh['sub'=32] {'sub'}, dimensions={0} | all-to-all | bytes 32768 | tf_op jit(solution)/shard_map/all_to_all | solution.py:707
  21.7 4.9 %coarse_columns.1 = f32[1536,128]{1,0:T(8,128)} custom-call(s32[32,128]{1,0:T(8,128)S(1)} %bitcast.37, f32[128,4096]{1,0:T(8,128)} %inverse_from.1), custom_call_target="tpu_custom_call" | custom-call | bytes 6000000 | tf_op jit(solution)/shard_map/coarse_columns/pallas_call | solution.py:48
  26.7 2.8 %all-to-all-start.2 = ((f32[32,48,128]{2,1,0:T(8,128)}), f32[32,48,128]{2,1,0:T(8,128)S(1)}, u32[]{:S(2)}, u32[]{:S(2)}) async-start(f32[32,48,128]{2,1,0:T(8,128)} %bitcast.11), calls=%async_computation.2 | async-start | bytes 1572864 | tf_op jit(solution)/shard_map/all_to_all | solution.py:724
  29.5 14.8 %products.1 = (bf16[1536,1024]{1,0:T(8,128)(2,1)}, bf16[1024,1024]{1,0:T(8,128)(2,1)}, bf16[96,1024]{1,0:T(8,128)(2,1)}, bf16[1024,256]{1,0:T(8,128)(2,1)}) custom-call(s32[1,1024]{1,0:T(1,128)S(1)} %get-tuple-element.151.row_ref, s32[1,1536]{1,0:T(1,128)S(1)} %copy-done.2, f32[48,1536]{1,0:T(8,128)S(1)} %bitcast.29, bf16[1536,1536]{1,0:T(8,128)(2,1)} %bitcast.44), custom_call_target="tpu_custom_call" | custom-call | bytes 30000000 | tf_op jit(solution)/shard_map/products/pallas_call | solution.py:48
  44.2 6.7 %residual_and_terms.1 = (f32[1536,128]{1,0:T(8,128)}, f32[1536,128]{1,0:T(8,128)}, f32[1024,128]{1,0:T(8,128)}, f32[896,128]{1,0:T(8,128)}) custom-call(f32[1536,128]{1,0:T(8,128)S(1)} %bitcast.28, f32[256,128]{1,0:T(8,128)S(1)} %collective-permute-done.a0, f32[256,128]{1,0:T(8,128)S(1)} %collective-permute-done.1.a1, ...), custom_call_target="tpu_custom_call" | custom-call | bytes 18000000 | tf_op jit(solution)/shard_map/residual_and_terms/pallas_call | solution.py:48
  50.9 6.9 %all-to-all-start.1 = ((f32[16,56,128]{2,1,0:T(8,128)}), f32[16,56,128]{2,1,0:T(8,128)S(1)}, u32[]{:S(2)}, u32[]{:S(2)}) async-start(f32[16,56,128]{2,1,0:T(8,128)} %bitcast.8), calls=%async_computation.1 | async-start | bytes 917504 | tf_op jit(solution)/shard_map/all_to_all | solution.py:785
  57.8 2.9 %coarse_block.1 = (f32[48,768]{1,0:T(8,128)S(1)}, f32[48,768]{1,0:T(8,128)S(1)}) custom-call(s32[32,128]{1,0:T(8,128)S(1)} %bitcast.38, s32[1]{0:T(128)} %bitcast.10.which_ref, f32[1536,128]{1,0:T(8,128)S(1)} %bitcast.26), custom_call_target="tpu_custom_call" | custom-call | bytes 6000000 | tf_op jit(solution)/shard_map/coarse_block/pallas_call | solution.py:48
  60.8 9.9 %local_products.1.local_place_from = bf16[1536,1024]{1,0:T(8,128)(2,1)} custom-call(s32[1,1024]{1,0:T(1,128)S(1)} %get-tuple-element.151.row_ref, s32[1,1536]{1,0:T(1,128)S(1)} %copy-done.2, f32[896,128]{1,0:T(8,128)} %get-tuple-element.157.after_ref, bf16[1536,1536]{1,0:T(8,128)(2,1)} %bitcast.42), custom_call_target="tpu_custom_call" | custom-call | bytes 30000000 | tf_op jit(solution)/shard_map/local_products/pallas_call | solution.py:48
  74.5 3.0 %collective-permute-start.6 = (f32[256,128]{1,0:T(8,128)S(1)}, f32[256,128]{1,0:T(8,128)S(1)}, u32[]{:S(2)}, u32[]{:S(2)}) collective-permute-start(f32[256,128]{1,0:T(8,128)S(1)} %get-tuple-element.170), channel_id=1, source_target_pairs={{0,24},{1,25},{2,26},{3,27},{4,28},{5,29},{6,30},{7,31},{8,16},{9,... | collective-permute-start | bytes 393224 | tf_op jit(solution)/shard_map/ppermute | solution.py:676
  81.4 4.2 %tables.1 = (bf16[1024,1536]{1,0:T(8,128)(2,1)S(1)}, bf16[1536,1024]{1,0:T(8,128)(2,1)S(1)}, f32[1536,128]{1,0:T(8,128)S(1)}, bf16[96,1536]{1,0:T(8,128)(2,1)S(1...) custom-call(s32[1,1024]{1,0:T(1,128)S(1)} %get-tuple-element.151.row, ...), custom_call_target="tpu_custom_call" | custom-call | bytes 15000000 | tf_op jit(solution)/shard_map/tables/pallas_call | solution.py:48
  92.3 4.5 %start.1 = (f32[1536,128]{1,0:T(8,128)S(1)}, f32[1536,128]{1,0:T(8,128)S(1)}, f32[48,128]{1,0:T(8,128)S(1)}, f32[8,128]{1,0:T(8,128)S(1)}, bf16[1536,1536]{1,0:T...) custom-call(f32[1536,128]{1,0:T(8,128)S(1)} %get-tuple-element.190.part_ref, f32[1536,128]{1,0:T(8,128)S(1)} %get-tuple-element.191.image_ref, ...), custom_call_target="tpu_custom_call" | custom-call | bytes 9000000 | tf_op jit(solution)/shard_map/start/pallas_call | solution.py:48
  99.3 17.3 %all_to_all.70 = f32[16,56,128]{2,1,0:T(8,128)S(1)} all-to-all(f32[16,56,128]{2,1,0:T(8,128)S(1)} %bitcast.35), channel_id=1, replica_groups={{0,2,4,6,8,10,12,14,16,18,20,22,24,26,28,30},{1,3,5,7,9,11,13,15,17,19,..., dimensions={0} | all-to-all | bytes 917504 | tf_op jit(solution)/shard_map/all_to_all | solution.py:785
  119.4 2.5 %collective-permute-start.15 = (f32[256,128]{1,0:T(8,128)S(1)}, f32[256,128]{1,0:T(8,128)S(1)}, u32[]{:S(2)}, u32[]{:S(2)}) collective-permute-start(f32[256,128]{1,0:T(8,128)S(1)} %get-tuple-element.211), channel_id=1, source_target_pairs={{0,24},{1,25},{2,26},{3,27},{4,28},{5,29},{6,30},{7,31},{8,16},{9,... | collective-permute-start | bytes 393224 | tf_op jit(solution)/shard_map/ppermute | solution.py:676
  122.0 2.5 %collective-permute-start.17 = (f32[256,128]{1,0:T(8,128)S(1)}, f32[256,128]{1,0:T(8,128)S(1)}, u32[]{:S(2)}, u32[]{:S(2)}) collective-permute-start(f32[256,128]{1,0:T(8,128)S(1)} %get-tuple-element.213), channel_id=1, source_target_pairs={{0,31},{1,2},{2,1},{3,4},{4,3},{5,6},{6,5},{7,8},{8,7},{9,10},{10,... | collective-permute-start | bytes 393224 | tf_op jit(solution)/shard_map/ppermute | solution.py:676
  127.3 3.4 %field_part.4 = (f32[1536,128]{1,0:T(8,128)S(1)}, f32[1536,128]{1,0:T(8,128)S(1)}, f32[1024,128]{1,0:T(8,128)S(1)}) custom-call(bf16[256,128]{1,0:T(8,128)(2,1)S(1)} %get-tuple-element.215.after_ref.values_ref, f32[1536,128]{1,0:T(8,128)S(1)} %get-tuple-element.217.local_ref, f32[1536,128]{1,0:T(8,128)S(1)} %get-tuple-element.180.weight_ref, ...), custom_call_target="tpu_custom_call" | custom-call | bytes 9000000 | tf_op jit(solution)/shard_map/field_part/pallas_call | solution.py:48
  131.9 2.5 %collective-permute-start.19 = (f32[256,128]{1,0:T(8,128)S(1)}, f32[256,128]{1,0:T(8,128)S(1)}, u32[]{:S(2)}, u32[]{:S(2)}) collective-permute-start(f32[256,128]{1,0:T(8,128)S(1)} %get-tuple-element.219), channel_id=1, source_target_pairs={{0,24},{1,25},{2,26},{3,27},{4,28},{5,29},{6,30},{7,31},{8,16},{9,... | collective-permute-start | bytes 393224 | tf_op jit(solution)/shard_map/ppermute | solution.py:676
  136.9 4.0 %first_update.1 = (f32[1536,128]{1,0:T(8,128)S(1)}, f32[1536,128]{1,0:T(8,128)S(1)}, f32[1536,128]{1,0:T(8,128)S(1)}, f32[1536,128]{1,0:T(8,128)S(1)}, f32[1536,...) custom-call(f32[1536,128]{1,0:T(8,128)S(1)} %get-tuple-element.223.part_ref, ...), custom_call_target="tpu_custom_call" | custom-call | bytes 12000000 | tf_op jit(solution)/shard_map/first_update/pallas_call | solution.py:48
  143.5 17.8 %all_to_all.71 = f32[16,56,128]{2,1,0:T(8,128)S(1)} all-to-all(f32[16,56,128]{2,1,0:T(8,128)S(1)} %bitcast.34), channel_id=1, replica_groups={{0,2,4,6,8,10,12,14,16,18,20,22,24,26,28,30},{1,3,5,7,9,11,13,15,17,19,..., dimensions={0} | all-to-all | bytes 917504 | tf_op jit(solution)/shard_map/all_to_all | solution.py:785
  171.5 3.4 %field_part.5 = (f32[1536,128]{1,0:T(8,128)S(1)}, f32[1536,128]{1,0:T(8,128)S(1)}, f32[1024,128]{1,0:T(8,128)S(1)}) custom-call(bf16[256,128]{1,0:T(8,128)(2,1)S(1)} %get-tuple-element.239.after_ref.values_ref, f32[1536,128]{1,0:T(8,128)S(1)} %get-tuple-element.242.local_ref, f32[1536,128]{1,0:T(8,128)S(1)} %get-tuple-element.180.weight_ref, ...), custom_call_target="tpu_custom_call" | custom-call | bytes 9000000 | tf_op jit(solution)/shard_map/field_part/pallas_call | solution.py:48
  181.5 2.6 %second_update.1 = (f32[32,512]{1,0:T(8,128)S(1)}, f32[8,128]{1,0:T(8,128)S(1)}, f32[1536,128]{1,0:T(8,128)S(1)}, f32[1536,128]{1,0:T(8,128)S(1)}, f32[1536,128]...) custom-call(f32[1536,128]{1,0:T(8,128)S(1)} %get-tuple-element.243.part_ref, ...), custom_call_target="tpu_custom_call" | custom-call | bytes 12000000 | tf_op jit(solution)/shard_map/second_update/pallas_call | solution.py:48
  184.7 3.1 %collective-permute-done.30.a2 = f32[256,128]{1,0:T(8,128)S(1)} collective-permute-done((f32[256,128]{1,0:T(8,128)S(1)}, f32[256,128]{1,0:T(8,128)S(1)}, u32[]{:S(2)}, u32[]{:S(2)}) %collective-permute-start.30) | collective-permute-done | bytes 131104 | tf_op jit(solution)/shard_map/ppermute | solution.py:676
  187.9 10.4 %all_to_all.72 = f32[32,1,512]{2,1,0:T(1,128)S(1)} all-to-all(f32[32,1,512]{2,1,0:T(1,128)S(1)} %copy.11), channel_id=1, replica_groups=mesh['sub'=32] {'sub'}, dimensions={0} | all-to-all | bytes 131072 | tf_op jit(solution)/shard_map/all_to_all | solution.py:966
  (89 shorter events, 52.1 us)
Async XLA Ops:
  3.6 18.1 %collective-permute-start = (f32[256,128]{1,0:T(8,128)S(1)}, f32[256,128]{1,0:T(8,128)S(1)}, u32[]{:S(2)}, u32[]{:S(2)}) collective-permute-start(f32[256,128]{1,0:T(8,128)S(1)} %get-tuple-element.143), channel_id=1, source_target_pairs={{0,24},{1,25},{2,26},{3,27},{4,28},{5,29},{6,30},{7,31},{8,16},{9,... | collective-permute-start | bytes 393224 | tf_op jit(solution)/shard_map/ppermute | solution.py:676
  8.7 12.9 %collective-permute-start.1 = (f32[256,128]{1,0:T(8,128)S(1)}, f32[256,128]{1,0:T(8,128)S(1)}, u32[]{:S(2)}, u32[]{:S(2)}) collective-permute-start(f32[256,128]{1,0:T(8,128)S(1)} %get-tuple-element.144), channel_id=1, source_target_pairs={{0,1},{1,0},{2,3},{3,2},{4,5},{5,4},{6,7},{7,6},{8,9},{9,8},{10,11... | collective-permute-start | bytes 393224 | tf_op jit(solution)/shard_map/ppermute | solution.py:676
  8.8 12.9 %collective-permute-start.2 = (f32[256,128]{1,0:T(8,128)S(1)}, f32[256,128]{1,0:T(8,128)S(1)}, u32[]{:S(2)}, u32[]{:S(2)}) collective-permute-start(f32[256,128]{1,0:T(8,128)S(1)} %get-tuple-element.145), channel_id=1, source_target_pairs={{0,31},{1,2},{2,1},{3,4},{4,3},{5,6},{6,5},{7,8},{8,7},{9,10},{10,... | collective-permute-start | bytes 393224 | tf_op jit(solution)/shard_map/ppermute | solution.py:676
  11.0 10.7 %collective-permute-start.3 = (f32[256,128]{1,0:T(8,128)S(1)}, f32[256,128]{1,0:T(8,128)S(1)}, u32[]{:S(2)}, u32[]{:S(2)}) collective-permute-start(f32[256,128]{1,0:T(8,128)S(1)} %get-tuple-element.146), channel_id=1, source_target_pairs={{0,8},{1,9},{2,10},{3,11},{4,12},{5,13},{6,14},{7,15},{8,0},{9,1},... | collective-permute-start | bytes 393224 | tf_op jit(solution)/shard_map/ppermute | solution.py:676
  26.7 24.3 %all-to-all-start.2 = ((f32[32,48,128]{2,1,0:T(8,128)}), f32[32,48,128]{2,1,0:T(8,128)S(1)}, u32[]{:S(2)}, u32[]{:S(2)}) async-start(f32[32,48,128]{2,1,0:T(8,128)} %bitcast.11), calls=%async_computation.2 | async-start | bytes 1572864 | tf_op jit(solution)/shard_map/all_to_all | solution.py:724
  50.9 21.1 %all-to-all-start.1 = ((f32[16,56,128]{2,1,0:T(8,128)}), f32[16,56,128]{2,1,0:T(8,128)S(1)}, u32[]{:S(2)}, u32[]{:S(2)}) async-start(f32[16,56,128]{2,1,0:T(8,128)} %bitcast.8), calls=%async_computation.1 | async-start | bytes 917504 | tf_op jit(solution)/shard_map/all_to_all | solution.py:785
  60.8 11.2 %collective-permute-start.4 = (f32[48,768]{1,0:T(8,128)S(1)}, f32[48,768]{1,0:T(8,128)S(1)}, u32[]{:S(2)}, u32[]{:S(2)}) collective-permute-start(f32[48,768]{1,0:T(8,128)S(1)} %get-tuple-element.161), channel_id=1, source_target_pairs={{0,1},{1,0},{2,3},{3,2},{4,5},{5,4},{6,7},{7,6},{8,9},{9,8},{10,11... | collective-permute-start | bytes 442376 | tf_op jit(solution)/shard_map/ppermute | solution.py:782
  74.5 13.5 %collective-permute-start.6 = (f32[256,128]{1,0:T(8,128)S(1)}, f32[256,128]{1,0:T(8,128)S(1)}, u32[]{:S(2)}, u32[]{:S(2)}) collective-permute-start(f32[256,128]{1,0:T(8,128)S(1)} %get-tuple-element.170), channel_id=1, source_target_pairs={{0,24},{1,25},{2,26},{3,27},{4,28},{5,29},{6,30},{7,31},{8,16},{9,... | collective-permute-start | bytes 393224 | tf_op jit(solution)/shard_map/ppermute | solution.py:676
  77.5 10.5 %collective-permute-start.7 = (f32[256,128]{1,0:T(8,128)S(1)}, f32[256,128]{1,0:T(8,128)S(1)}, u32[]{:S(2)}, u32[]{:S(2)}) collective-permute-start(f32[256,128]{1,0:T(8,128)S(1)} %get-tuple-element.171), channel_id=1, source_target_pairs={{0,1},{1,0},{2,3},{3,2},{4,5},{5,4},{6,7},{7,6},{8,9},{9,8},{10,11... | collective-permute-start | bytes 393224 | tf_op jit(solution)/shard_map/ppermute | solution.py:676
  77.5 10.5 %collective-permute-start.8 = (f32[256,128]{1,0:T(8,128)S(1)}, f32[256,128]{1,0:T(8,128)S(1)}, u32[]{:S(2)}, u32[]{:S(2)}) collective-permute-start(f32[256,128]{1,0:T(8,128)S(1)} %get-tuple-element.172), channel_id=1, source_target_pairs={{0,31},{1,2},{2,1},{3,4},{4,3},{5,6},{6,5},{7,8},{8,7},{9,10},{10,... | collective-permute-start | bytes 393224 | tf_op jit(solution)/shard_map/ppermute | solution.py:676
  88.7 10.3 %collective-permute-start.10 = (f32[256,128]{1,0:T(8,128)S(1)}, f32[256,128]{1,0:T(8,128)S(1)}, u32[]{:S(2)}, u32[]{:S(2)}) collective-permute-start(f32[256,128]{1,0:T(8,128)S(1)} %get-tuple-element.186), channel_id=1, source_target_pairs={{0,24},{1,25},{2,26},{3,27},{4,28},{5,29},{6,30},{7,31},{8,16},{9,... | collective-permute-start | bytes 393224 | tf_op jit(solution)/shard_map/ppermute | solution.py:676
  89.8 9.2 %collective-permute-start.11 = (f32[256,128]{1,0:T(8,128)S(1)}, f32[256,128]{1,0:T(8,128)S(1)}, u32[]{:S(2)}, u32[]{:S(2)}) collective-permute-start(f32[256,128]{1,0:T(8,128)S(1)} %get-tuple-element.187), channel_id=1, source_target_pairs={{0,1},{1,0},{2,3},{3,2},{4,5},{5,4},{6,7},{7,6},{8,9},{9,8},{10,11... | collective-permute-start | bytes 393224 | tf_op jit(solution)/shard_map/ppermute | solution.py:676
  89.8 9.2 %collective-permute-start.12 = (f32[256,128]{1,0:T(8,128)S(1)}, f32[256,128]{1,0:T(8,128)S(1)}, u32[]{:S(2)}, u32[]{:S(2)}) collective-permute-start(f32[256,128]{1,0:T(8,128)S(1)} %get-tuple-element.188), channel_id=1, source_target_pairs={{0,31},{1,2},{2,1},{3,4},{4,3},{5,6},{6,5},{7,8},{8,7},{9,10},{10,... | collective-permute-start | bytes 393224 | tf_op jit(solution)/shard_map/ppermute | solution.py:676
  119.4 11.3 %collective-permute-start.15 = (f32[256,128]{1,0:T(8,128)S(1)}, f32[256,128]{1,0:T(8,128)S(1)}, u32[]{:S(2)}, u32[]{:S(2)}) collective-permute-start(f32[256,128]{1,0:T(8,128)S(1)} %get-tuple-element.211), channel_id=1, source_target_pairs={{0,24},{1,25},{2,26},{3,27},{4,28},{5,29},{6,30},{7,31},{8,16},{9,... | collective-permute-start | bytes 393224 | tf_op jit(solution)/shard_map/ppermute | solution.py:676
  122.0 8.8 %collective-permute-start.16 = (f32[256,128]{1,0:T(8,128)S(1)}, f32[256,128]{1,0:T(8,128)S(1)}, u32[]{:S(2)}, u32[]{:S(2)}) collective-permute-start(f32[256,128]{1,0:T(8,128)S(1)} %get-tuple-element.212), channel_id=1, source_target_pairs={{0,1},{1,0},{2,3},{3,2},{4,5},{5,4},{6,7},{7,6},{8,9},{9,8},{10,11... | collective-permute-start | bytes 393224 | tf_op jit(solution)/shard_map/ppermute | solution.py:676
  122.0 9.0 %collective-permute-start.17 = (f32[256,128]{1,0:T(8,128)S(1)}, f32[256,128]{1,0:T(8,128)S(1)}, u32[]{:S(2)}, u32[]{:S(2)}) collective-permute-start(f32[256,128]{1,0:T(8,128)S(1)} %get-tuple-element.213), channel_id=1, source_target_pairs={{0,31},{1,2},{2,1},{3,4},{4,3},{5,6},{6,5},{7,8},{8,7},{9,10},{10,... | collective-permute-start | bytes 393224 | tf_op jit(solution)/shard_map/ppermute | solution.py:676
  131.9 11.3 %collective-permute-start.19 = (f32[256,128]{1,0:T(8,128)S(1)}, f32[256,128]{1,0:T(8,128)S(1)}, u32[]{:S(2)}, u32[]{:S(2)}) collective-permute-start(f32[256,128]{1,0:T(8,128)S(1)} %get-tuple-element.219), channel_id=1, source_target_pairs={{0,24},{1,25},{2,26},{3,27},{4,28},{5,29},{6,30},{7,31},{8,16},{9,... | collective-permute-start | bytes 393224 | tf_op jit(solution)/shard_map/ppermute | solution.py:676
  134.4 8.8 %collective-permute-start.20 = (f32[256,128]{1,0:T(8,128)S(1)}, f32[256,128]{1,0:T(8,128)S(1)}, u32[]{:S(2)}, u32[]{:S(2)}) collective-permute-start(f32[256,128]{1,0:T(8,128)S(1)} %get-tuple-element.220), channel_id=1, source_target_pairs={{0,1},{1,0},{2,3},{3,2},{4,5},{5,4},{6,7},{7,6},{8,9},{9,8},{10,11... | collective-permute-start | bytes 393224 | tf_op jit(solution)/shard_map/ppermute | solution.py:676
  134.4 8.8 %collective-permute-start.21 = (f32[256,128]{1,0:T(8,128)S(1)}, f32[256,128]{1,0:T(8,128)S(1)}, u32[]{:S(2)}, u32[]{:S(2)}) collective-permute-start(f32[256,128]{1,0:T(8,128)S(1)} %get-tuple-element.221), channel_id=1, source_target_pairs={{0,31},{1,2},{2,1},{3,4},{4,3},{5,6},{6,5},{7,8},{8,7},{9,10},{10,... | collective-permute-start | bytes 393224 | tf_op jit(solution)/shard_map/ppermute | solution.py:676
  163.7 11.2 %collective-permute-start.24 = (f32[256,128]{1,0:T(8,128)S(1)}, f32[256,128]{1,0:T(8,128)S(1)}, u32[]{:S(2)}, u32[]{:S(2)}) collective-permute-start(f32[256,128]{1,0:T(8,128)S(1)} %get-tuple-element.245), channel_id=1, source_target_pairs={{0,24},{1,25},{2,26},{3,27},{4,28},{5,29},{6,30},{7,31},{8,16},{9,... | collective-permute-start | bytes 393224 | tf_op jit(solution)/shard_map/ppermute | solution.py:676
  166.2 8.7 %collective-permute-start.25 = (f32[256,128]{1,0:T(8,128)S(1)}, f32[256,128]{1,0:T(8,128)S(1)}, u32[]{:S(2)}, u32[]{:S(2)}) collective-permute-start(f32[256,128]{1,0:T(8,128)S(1)} %get-tuple-element.246), channel_id=1, source_target_pairs={{0,1},{1,0},{2,3},{3,2},{4,5},{5,4},{6,7},{7,6},{8,9},{9,8},{10,11... | collective-permute-start | bytes 393224 | tf_op jit(solution)/shard_map/ppermute | solution.py:676
  166.4 9.0 %collective-permute-start.26 = (f32[256,128]{1,0:T(8,128)S(1)}, f32[256,128]{1,0:T(8,128)S(1)}, u32[]{:S(2)}, u32[]{:S(2)}) collective-permute-start(f32[256,128]{1,0:T(8,128)S(1)} %get-tuple-element.247), channel_id=1, source_target_pairs={{0,31},{1,2},{2,1},{3,4},{4,3},{5,6},{6,5},{7,8},{8,7},{9,10},{10,... | collective-permute-start | bytes 393224 | tf_op jit(solution)/shard_map/ppermute | solution.py:676
  176.6 8.2 %collective-permute-start.28 = (f32[256,128]{1,0:T(8,128)S(1)}, f32[256,128]{1,0:T(8,128)S(1)}, u32[]{:S(2)}, u32[]{:S(2)}) collective-permute-start(f32[256,128]{1,0:T(8,128)S(1)} %get-tuple-element.260), channel_id=1, source_target_pairs={{0,24},{1,25},{2,26},{3,27},{4,28},{5,29},{6,30},{7,31},{8,16},{9,... | collective-permute-start | bytes 393224 | tf_op jit(solution)/shard_map/ppermute | solution.py:676
  179.0 8.8 %collective-permute-start.30 = (f32[256,128]{1,0:T(8,128)S(1)}, f32[256,128]{1,0:T(8,128)S(1)}, u32[]{:S(2)}, u32[]{:S(2)}) collective-permute-start(f32[256,128]{1,0:T(8,128)S(1)} %get-tuple-element.262), channel_id=1, source_target_pairs={{0,31},{1,2},{2,1},{3,4},{4,3},{5,6},{6,5},{7,8},{8,7},{9,10},{10,... | collective-permute-start | bytes 393224 | tf_op jit(solution)/shard_map/ppermute | solution.py:676
  (13 other events, 127.7 us)

commit v3 on v2

--- a/solution.py
+++ b/solution.py
@@ -224,15 +224,15 @@
     copy.wait()
 
     def product(lo):
-        at = pl.ds(lo, FINE)
+        at = pl.ds(lo, TILE)
         stiff_place_ref[at, :] = dot(stiff[at, :], place[...]).astype(BF16)
 
     def shared(lo):
-        at = pl.ds(lo, FINE)
+        at = pl.ds(lo, TILE)
         stiff_shared_ref[at, :] = dot(pick[at, :], stiff_place_ref[...]).astype(BF16)
 
-    each(stiff.shape[0], FINE, product)
-    each(pick.shape[0], FINE, shared)
+    each(stiff.shape[0], TILE, product)
+    each(pick.shape[0], TILE, shared)
 
 
 def local_products_kernel(row_ref, count_ref, after_ref, inverse_from, local_place_ref,
@@ -246,10 +246,10 @@
         copy.wait()
 
     def product(lo):
-        at = pl.ds(lo, FINE)
+        at = pl.ds(lo, TILE)
         local_place_ref[at, :] = (dot(inverse[at, :], place[...]) * listed).astype(BF16)
 
-    each(rows, FINE, product)
+    each(rows, TILE, product)
 
 
 def tables_kernel(row_ref, count_ref, basis_ref, after_ref, stiff_from, stiff_place_from,
@@ -338,7 +338,7 @@
 
 
 def send_terms(terms, scalars, send_ref):
-    block = jnp.concatenate([terms, scalars], axis=0)
+    block = terms if scalars is None else jnp.concatenate([terms, scalars], axis=0)
     rows = block.shape[0]
     for g in range(send_ref.shape[0] // rows):
         send_ref[g * rows : (g + 1) * rows, :] = block
@@ -379,19 +379,21 @@
         both = pair(weight[at, :] * resid)
         cat[at, :] = both
         terms += dot(basis2[:, at], both)
-    send_terms(three(terms, ncl), jnp.zeros((SCAL, rhs), F32), send_ref)
+    send_terms(three(terms, ncl), None, send_ref)
     fill_pick(row_ref, pick)
     copy.wait()
     front(inverse, weight, pick, cat, local_ref, pre_ref, cat2)
 
 
-def coarse_solve_kernel(got_ref, g_ref, own_ref, other_ref):
+def coarse_solve_kernel(extra, got_ref, g_ref, own_ref, other_ref):
     ncl = g_ref.shape[0] // 4
-    rows = ncl + SCAL
+    rows = ncl + extra
     groups = got_ref.shape[0] // rows
     got = got_ref[...].reshape(groups, rows, got_ref.shape[1])
     terms = got[:, :ncl].reshape(groups * ncl, got_ref.shape[1])
-    scalars = jnp.sum(got[:, ncl:], axis=0)
+    scalars = jnp.zeros((SCAL, got_ref.shape[1]), F32)
+    if extra:
+        scalars = jnp.sum(got[:, ncl:], axis=0)
     values = three(dot(g_ref[...], pair(terms)), 2 * ncl)
     own_ref[:ncl, :] = values[:ncl]
     own_ref[ncl:, :] = scalars
@@ -727,7 +729,7 @@
         first_kernel,
         "residual_and_terms",
         (loads[0], *arrived, listed, counts, basis, inverse),
-        [away(fields), away(fields), away((lists, rhs)), far((groups * block, rhs))],
+        [away(fields), away(fields), away((lists, rhs)), far((groups * ncl, rhs))],
         [
             wide,
             wide_arr,
@@ -829,7 +831,7 @@
 
     def correct(terms, pre, bring_in=None):
         own, other = call(
-            coarse_solve_kernel,
+            functools.partial(coarse_solve_kernel, 0 if bring_in else SCAL),
             "coarse_solve",
             (terms, coarse),
             [far((block, rhs)), far((block, rhs))],

time: 201 us -> 200 us (level)
  transfers between devices with their start and end apart: 34 -> 34, of which waited for: 7 -> 8; matrix products, arithmetic and copies ran while one was open for 0% -> 0% of each run, Pallas kernels for 36% -> 36%
where the time goes in v3:
time: 200 us; the launch traced here: 199 us
  Pallas kernels  85.6 us (43%)
  blocking collectives  54.3 us (27%)
  starting transfers between devices  51.9 us (26%)
  waiting for transfers between devices  5.71 us (3%)
    pallas_call x33, Pallas kernels, call(): pl.pallas_call(kernel, name=name, out_shape=tuple(outs), in_specs=[specs....  85.6 us
    ppermute x28, starting transfers between devices, exchange(): return [lax.ppermute(out, 'sub', swap) for out, swap in zip(outs, swaps)]  41.8 us
    all_to_all x2, blocking collectives, share(): lax.all_to_all(send, 'sub', 0, 0, tiled=True, axis_index_groups=cores)  35 us
    all_to_all x1, blocking collectives, body(): sums = lax.all_to_all(send, 'sub', 0, 0, tiled=True)  10.4 us
    all_to_all x1, blocking collectives, body(): maps = lax.all_to_all(maps, 'sub', 0, 0, tiled=True)  8.92 us
    all_to_all x1, starting transfers between devices, share(): lax.all_to_all(send, 'sub', 0, 0, tiled=True, axis_index_groups=cores)  6.68 us
    ppermute x28, waiting for transfers between devices, exchange(): return [lax.ppermute(out, 'sub', swap) for out, swap in zip(outs, swaps)]  5.03 us
  transfers between devices with their start and end apart: 34, of which 8 were waited for; matrix products, arithmetic and copies ran while one was open for 0% of the time, Pallas kernels for 36%

profile of v3, /device:TPU:0, one launch (start us, length us, event | category | flops | bytes accessed | tf_op | source)
XLA Modules:
  0.0 198.9 jit_solution(9277853298401143440)
XLA Ops:
  0.7 3.0 %loads.1 = (s32[1,1024]{1,0:T(1,128)S(1)}, s32[32,128]{1,0:T(8,128)S(1)}, f32[256,128]{1,0:T(8,128)S(1)}, f32[256,128]{1,0:T(8,128)S(1)}, f32[256,128]{1,0:T(8,128)S(1)}, /*index=5*/f32[256,128]{1,0:T(8,128)S(1)}) custom-call(s32[4,256]{1,0:T(4,128)} %bitcast.46, f32[1536,128]{1,0:T(8,128)} %bitcast.27, s32[1,48]{1,0:T(1,128)} %map_from.1), custom_call_target="tpu_custom_call" | custom-call | bytes 6000000 | tf_op jit(solution)/shard_map/loads/pallas_call | solution.py:48
  3.6 5.1 %collective-permute-start = (f32[256,128]{1,0:T(8,128)S(1)}, f32[256,128]{1,0:T(8,128)S(1)}, u32[]{:S(2)}, u32[]{:S(2)}) collective-permute-start(f32[256,128]{1,0:T(8,128)S(1)} %get-tuple-element.143), channel_id=1, source_target_pairs={{0,24},{1,25},{2,26},{3,27},{4,28},{5,29},{6,30},{7,31},{8,16},{9,... | collective-permute-start | bytes 393224 | tf_op jit(solution)/shard_map/ppermute | solution.py:678
  12.8 8.9 %all_to_all.69 = s32[32,1,128]{2,1,0:T(1,128)S(1)} all-to-all(s32[32,1,128]{2,1,0:T(1,128)S(1)} %bitcast.40), channel_id=1, replica_groups=mesh['sub'=32] {'sub'}, dimensions={0} | all-to-all | bytes 32768 | tf_op jit(solution)/shard_map/all_to_all | solution.py:709
  21.7 4.9 %coarse_columns.1 = f32[1536,128]{1,0:T(8,128)} custom-call(s32[32,128]{1,0:T(8,128)S(1)} %bitcast.37, f32[128,4096]{1,0:T(8,128)} %inverse_from.1), custom_call_target="tpu_custom_call" | custom-call | bytes 6000000 | tf_op jit(solution)/shard_map/coarse_columns/pallas_call | solution.py:48
  26.7 2.8 %all-to-all-start.2 = ((f32[32,48,128]{2,1,0:T(8,128)}), f32[32,48,128]{2,1,0:T(8,128)S(1)}, u32[]{:S(2)}, u32[]{:S(2)}) async-start(f32[32,48,128]{2,1,0:T(8,128)} %bitcast.11), calls=%async_computation.2 | async-start | bytes 1572864 | tf_op jit(solution)/shard_map/all_to_all | solution.py:726
  29.5 13.7 %products.1 = (bf16[1536,1024]{1,0:T(8,128)(2,1)}, bf16[1024,1024]{1,0:T(8,128)(2,1)}, bf16[96,1024]{1,0:T(8,128)(2,1)}, bf16[1024,256]{1,0:T(8,128)(2,1)}) custom-call(s32[1,1024]{1,0:T(1,128)S(1)} %get-tuple-element.151.row_ref, s32[1,1536]{1,0:T(1,128)S(1)} %copy-done.2, f32[48,1536]{1,0:T(8,128)S(1)} %bitcast.29, bf16[1536,1536]{1,0:T(8,128)(2,1)} %bitcast.44), custom_call_target="tpu_custom_call" | custom-call | bytes 30000000 | tf_op jit(solution)/shard_map/products/pallas_call | solution.py:48
  43.2 6.6 %residual_and_terms.1 = (f32[1536,128]{1,0:T(8,128)}, f32[1536,128]{1,0:T(8,128)}, f32[1024,128]{1,0:T(8,128)}, f32[768,128]{1,0:T(8,128)}) custom-call(f32[1536,128]{1,0:T(8,128)S(1)} %bitcast.28, f32[256,128]{1,0:T(8,128)S(1)} %collective-permute-done.a0, f32[256,128]{1,0:T(8,128)S(1)} %collective-permute-done.1.a1, ...), custom_call_target="tpu_custom_call" | custom-call | bytes 18000000 | tf_op jit(solution)/shard_map/residual_and_terms/pallas_call | solution.py:48
  50.0 6.7 %all-to-all-start.1 = ((f32[16,48,128]{2,1,0:T(8,128)}), f32[16,48,128]{2,1,0:T(8,128)S(1)}, u32[]{:S(2)}, u32[]{:S(2)}) async-start(f32[16,48,128]{2,1,0:T(8,128)} %bitcast.8), calls=%async_computation.1 | async-start | bytes 786432 | tf_op jit(solution)/shard_map/all_to_all | solution.py:787
  56.7 2.9 %coarse_block.1 = (f32[48,768]{1,0:T(8,128)S(1)}, f32[48,768]{1,0:T(8,128)S(1)}) custom-call(s32[32,128]{1,0:T(8,128)S(1)} %bitcast.38, s32[1]{0:T(128)} %bitcast.10.which_ref, f32[1536,128]{1,0:T(8,128)S(1)} %bitcast.26), custom_call_target="tpu_custom_call" | custom-call | bytes 6000000 | tf_op jit(solution)/shard_map/coarse_block/pallas_call | solution.py:48
  59.8 9.4 %local_products.1.local_place_from = bf16[1536,1024]{1,0:T(8,128)(2,1)} custom-call(s32[1,1024]{1,0:T(1,128)S(1)} %get-tuple-element.151.row_ref, s32[1,1536]{1,0:T(1,128)S(1)} %copy-done.2, f32[768,128]{1,0:T(8,128)} %get-tuple-element.157.after_ref, bf16[1536,1536]{1,0:T(8,128)(2,1)} %bitcast.42), custom_call_target="tpu_custom_call" | custom-call | bytes 30000000 | tf_op jit(solution)/shard_map/local_products/pallas_call | solution.py:48
  72.2 3.7 %collective-permute-start.6 = (f32[256,128]{1,0:T(8,128)S(1)}, f32[256,128]{1,0:T(8,128)S(1)}, u32[]{:S(2)}, u32[]{:S(2)}) collective-permute-start(f32[256,128]{1,0:T(8,128)S(1)} %get-tuple-element.170), channel_id=1, source_target_pairs={{0,24},{1,25},{2,26},{3,27},{4,28},{5,29},{6,30},{7,31},{8,16},{9,... | collective-permute-start | bytes 393224 | tf_op jit(solution)/shard_map/ppermute | solution.py:678
  79.8 4.2 %tables.1 = (bf16[1024,1536]{1,0:T(8,128)(2,1)S(1)}, bf16[1536,1024]{1,0:T(8,128)(2,1)S(1)}, f32[1536,128]{1,0:T(8,128)S(1)}, bf16[96,1536]{1,0:T(8,128)(2,1)S(1...) custom-call(s32[1,1024]{1,0:T(1,128)S(1)} %get-tuple-element.151.row, ...), custom_call_target="tpu_custom_call" | custom-call | bytes 15000000 | tf_op jit(solution)/shard_map/tables/pallas_call | solution.py:48
  90.8 4.5 %start.1 = (f32[1536,128]{1,0:T(8,128)S(1)}, f32[1536,128]{1,0:T(8,128)S(1)}, f32[48,128]{1,0:T(8,128)S(1)}, f32[8,128]{1,0:T(8,128)S(1)}, bf16[1536,1536]{1,0:T...) custom-call(f32[1536,128]{1,0:T(8,128)S(1)} %get-tuple-element.190.part_ref, f32[1536,128]{1,0:T(8,128)S(1)} %get-tuple-element.191.image_ref, ...), custom_call_target="tpu_custom_call" | custom-call | bytes 9000000 | tf_op jit(solution)/shard_map/start/pallas_call | solution.py:48
  97.8 17.2 %all_to_all.70 = f32[16,56,128]{2,1,0:T(8,128)S(1)} all-to-all(f32[16,56,128]{2,1,0:T(8,128)S(1)} %bitcast.35), channel_id=1, replica_groups={{0,2,4,6,8,10,12,14,16,18,20,22,24,26,28,30},{1,3,5,7,9,11,13,15,17,19,..., dimensions={0} | all-to-all | bytes 917504 | tf_op jit(solution)/shard_map/all_to_all | solution.py:787
  117.8 2.5 %collective-permute-start.15 = (f32[256,128]{1,0:T(8,128)S(1)}, f32[256,128]{1,0:T(8,128)S(1)}, u32[]{:S(2)}, u32[]{:S(2)}) collective-permute-start(f32[256,128]{1,0:T(8,128)S(1)} %get-tuple-element.211), channel_id=1, source_target_pairs={{0,24},{1,25},{2,26},{3,27},{4,28},{5,29},{6,30},{7,31},{8,16},{9,... | collective-permute-start | bytes 393224 | tf_op jit(solution)/shard_map/ppermute | solution.py:678
  120.4 2.5 %collective-permute-start.17 = (f32[256,128]{1,0:T(8,128)S(1)}, f32[256,128]{1,0:T(8,128)S(1)}, u32[]{:S(2)}, u32[]{:S(2)}) collective-permute-start(f32[256,128]{1,0:T(8,128)S(1)} %get-tuple-element.213), channel_id=1, source_target_pairs={{0,31},{1,2},{2,1},{3,4},{4,3},{5,6},{6,5},{7,8},{8,7},{9,10},{10,... | collective-permute-start | bytes 393224 | tf_op jit(solution)/shard_map/ppermute | solution.py:678
  125.7 3.4 %field_part.4 = (f32[1536,128]{1,0:T(8,128)S(1)}, f32[1536,128]{1,0:T(8,128)S(1)}, f32[1024,128]{1,0:T(8,128)S(1)}) custom-call(bf16[256,128]{1,0:T(8,128)(2,1)S(1)} %get-tuple-element.215.after_ref.values_ref, f32[1536,128]{1,0:T(8,128)S(1)} %get-tuple-element.217.local_ref, f32[1536,128]{1,0:T(8,128)S(1)} %get-tuple-element.180.weight_ref, ...), custom_call_target="tpu_custom_call" | custom-call | bytes 9000000 | tf_op jit(solution)/shard_map/field_part/pallas_call | solution.py:48
  130.3 2.5 %collective-permute-start.19 = (f32[256,128]{1,0:T(8,128)S(1)}, f32[256,128]{1,0:T(8,128)S(1)}, u32[]{:S(2)}, u32[]{:S(2)}) collective-permute-start(f32[256,128]{1,0:T(8,128)S(1)} %get-tuple-element.219), channel_id=1, source_target_pairs={{0,24},{1,25},{2,26},{3,27},{4,28},{5,29},{6,30},{7,31},{8,16},{9,... | collective-permute-start | bytes 393224 | tf_op jit(solution)/shard_map/ppermute | solution.py:678
  135.4 4.0 %first_update.1 = (f32[1536,128]{1,0:T(8,128)S(1)}, f32[1536,128]{1,0:T(8,128)S(1)}, f32[1536,128]{1,0:T(8,128)S(1)}, f32[1536,128]{1,0:T(8,128)S(1)}, f32[1536,...) custom-call(f32[1536,128]{1,0:T(8,128)S(1)} %get-tuple-element.223.part_ref, ...), custom_call_target="tpu_custom_call" | custom-call | bytes 12000000 | tf_op jit(solution)/shard_map/first_update/pallas_call | solution.py:48
  141.9 17.8 %all_to_all.71 = f32[16,56,128]{2,1,0:T(8,128)S(1)} all-to-all(f32[16,56,128]{2,1,0:T(8,128)S(1)} %bitcast.34), channel_id=1, replica_groups={{0,2,4,6,8,10,12,14,16,18,20,22,24,26,28,30},{1,3,5,7,9,11,13,15,17,19,..., dimensions={0} | all-to-all | bytes 917504 | tf_op jit(solution)/shard_map/all_to_all | solution.py:787
  169.9 3.4 %field_part.5 = (f32[1536,128]{1,0:T(8,128)S(1)}, f32[1536,128]{1,0:T(8,128)S(1)}, f32[1024,128]{1,0:T(8,128)S(1)}) custom-call(bf16[256,128]{1,0:T(8,128)(2,1)S(1)} %get-tuple-element.239.after_ref.values_ref, f32[1536,128]{1,0:T(8,128)S(1)} %get-tuple-element.242.local_ref, f32[1536,128]{1,0:T(8,128)S(1)} %get-tuple-element.180.weight_ref, ...), custom_call_target="tpu_custom_call" | custom-call | bytes 9000000 | tf_op jit(solution)/shard_map/field_part/pallas_call | solution.py:48
  179.9 2.6 %second_update.1 = (f32[32,512]{1,0:T(8,128)S(1)}, f32[8,128]{1,0:T(8,128)S(1)}, f32[1536,128]{1,0:T(8,128)S(1)}, f32[1536,128]{1,0:T(8,128)S(1)}, f32[1536,128]...) custom-call(f32[1536,128]{1,0:T(8,128)S(1)} %get-tuple-element.243.part_ref, ...), custom_call_target="tpu_custom_call" | custom-call | bytes 12000000 | tf_op jit(solution)/shard_map/second_update/pallas_call | solution.py:48
  183.1 3.1 %collective-permute-done.30.a2 = f32[256,128]{1,0:T(8,128)S(1)} collective-permute-done((f32[256,128]{1,0:T(8,128)S(1)}, f32[256,128]{1,0:T(8,128)S(1)}, u32[]{:S(2)}, u32[]{:S(2)}) %collective-permute-start.30) | collective-permute-done | bytes 131104 | tf_op jit(solution)/shard_map/ppermute | solution.py:678
  186.3 10.4 %all_to_all.72 = f32[32,1,512]{2,1,0:T(1,128)S(1)} all-to-all(f32[32,1,512]{2,1,0:T(1,128)S(1)} %copy.11), channel_id=1, replica_groups=mesh['sub'=32] {'sub'}, dimensions={0} | all-to-all | bytes 131072 | tf_op jit(solution)/shard_map/all_to_all | solution.py:968
  (89 shorter events, 51.7 us)
Async XLA Ops:
  3.6 18.1 %collective-permute-start = (f32[256,128]{1,0:T(8,128)S(1)}, f32[256,128]{1,0:T(8,128)S(1)}, u32[]{:S(2)}, u32[]{:S(2)}) collective-permute-start(f32[256,128]{1,0:T(8,128)S(1)} %get-tuple-element.143), channel_id=1, source_target_pairs={{0,24},{1,25},{2,26},{3,27},{4,28},{5,29},{6,30},{7,31},{8,16},{9,... | collective-permute-start | bytes 393224 | tf_op jit(solution)/shard_map/ppermute | solution.py:678
  8.7 12.9 %collective-permute-start.1 = (f32[256,128]{1,0:T(8,128)S(1)}, f32[256,128]{1,0:T(8,128)S(1)}, u32[]{:S(2)}, u32[]{:S(2)}) collective-permute-start(f32[256,128]{1,0:T(8,128)S(1)} %get-tuple-element.144), channel_id=1, source_target_pairs={{0,1},{1,0},{2,3},{3,2},{4,5},{5,4},{6,7},{7,6},{8,9},{9,8},{10,11... | collective-permute-start | bytes 393224 | tf_op jit(solution)/shard_map/ppermute | solution.py:678
  8.8 12.9 %collective-permute-start.2 = (f32[256,128]{1,0:T(8,128)S(1)}, f32[256,128]{1,0:T(8,128)S(1)}, u32[]{:S(2)}, u32[]{:S(2)}) collective-permute-start(f32[256,128]{1,0:T(8,128)S(1)} %get-tuple-element.145), channel_id=1, source_target_pairs={{0,31},{1,2},{2,1},{3,4},{4,3},{5,6},{6,5},{7,8},{8,7},{9,10},{10,... | collective-permute-start | bytes 393224 | tf_op jit(solution)/shard_map/ppermute | solution.py:678
  11.0 10.7 %collective-permute-start.3 = (f32[256,128]{1,0:T(8,128)S(1)}, f32[256,128]{1,0:T(8,128)S(1)}, u32[]{:S(2)}, u32[]{:S(2)}) collective-permute-start(f32[256,128]{1,0:T(8,128)S(1)} %get-tuple-element.146), channel_id=1, source_target_pairs={{0,8},{1,9},{2,10},{3,11},{4,12},{5,13},{6,14},{7,15},{8,0},{9,1},... | collective-permute-start | bytes 393224 | tf_op jit(solution)/shard_map/ppermute | solution.py:678
  26.7 23.4 %all-to-all-start.2 = ((f32[32,48,128]{2,1,0:T(8,128)}), f32[32,48,128]{2,1,0:T(8,128)S(1)}, u32[]{:S(2)}, u32[]{:S(2)}) async-start(f32[32,48,128]{2,1,0:T(8,128)} %bitcast.11), calls=%async_computation.2 | async-start | bytes 1572864 | tf_op jit(solution)/shard_map/all_to_all | solution.py:726
  50.0 19.6 %all-to-all-start.1 = ((f32[16,48,128]{2,1,0:T(8,128)}), f32[16,48,128]{2,1,0:T(8,128)S(1)}, u32[]{:S(2)}, u32[]{:S(2)}) async-start(f32[16,48,128]{2,1,0:T(8,128)} %bitcast.8), calls=%async_computation.1 | async-start | bytes 786432 | tf_op jit(solution)/shard_map/all_to_all | solution.py:787
  59.7 10.0 %collective-permute-start.4 = (f32[48,768]{1,0:T(8,128)S(1)}, f32[48,768]{1,0:T(8,128)S(1)}, u32[]{:S(2)}, u32[]{:S(2)}) collective-permute-start(f32[48,768]{1,0:T(8,128)S(1)} %get-tuple-element.161), channel_id=1, source_target_pairs={{0,1},{1,0},{2,3},{3,2},{4,5},{5,4},{6,7},{7,6},{8,9},{9,8},{10,11... | collective-permute-start | bytes 442376 | tf_op jit(solution)/shard_map/ppermute | solution.py:784
  72.2 14.2 %collective-permute-start.6 = (f32[256,128]{1,0:T(8,128)S(1)}, f32[256,128]{1,0:T(8,128)S(1)}, u32[]{:S(2)}, u32[]{:S(2)}) collective-permute-start(f32[256,128]{1,0:T(8,128)S(1)} %get-tuple-element.170), channel_id=1, source_target_pairs={{0,24},{1,25},{2,26},{3,27},{4,28},{5,29},{6,30},{7,31},{8,16},{9,... | collective-permute-start | bytes 393224 | tf_op jit(solution)/shard_map/ppermute | solution.py:678
  75.9 10.5 %collective-permute-start.7 = (f32[256,128]{1,0:T(8,128)S(1)}, f32[256,128]{1,0:T(8,128)S(1)}, u32[]{:S(2)}, u32[]{:S(2)}) collective-permute-start(f32[256,128]{1,0:T(8,128)S(1)} %get-tuple-element.171), channel_id=1, source_target_pairs={{0,1},{1,0},{2,3},{3,2},{4,5},{5,4},{6,7},{7,6},{8,9},{9,8},{10,11... | collective-permute-start | bytes 393224 | tf_op jit(solution)/shard_map/ppermute | solution.py:678
  75.9 10.5 %collective-permute-start.8 = (f32[256,128]{1,0:T(8,128)S(1)}, f32[256,128]{1,0:T(8,128)S(1)}, u32[]{:S(2)}, u32[]{:S(2)}) collective-permute-start(f32[256,128]{1,0:T(8,128)S(1)} %get-tuple-element.172), channel_id=1, source_target_pairs={{0,31},{1,2},{2,1},{3,4},{4,3},{5,6},{6,5},{7,8},{8,7},{9,10},{10,... | collective-permute-start | bytes 393224 | tf_op jit(solution)/shard_map/ppermute | solution.py:678
  87.1 10.4 %collective-permute-start.10 = (f32[256,128]{1,0:T(8,128)S(1)}, f32[256,128]{1,0:T(8,128)S(1)}, u32[]{:S(2)}, u32[]{:S(2)}) collective-permute-start(f32[256,128]{1,0:T(8,128)S(1)} %get-tuple-element.186), channel_id=1, source_target_pairs={{0,24},{1,25},{2,26},{3,27},{4,28},{5,29},{6,30},{7,31},{8,16},{9,... | collective-permute-start | bytes 393224 | tf_op jit(solution)/shard_map/ppermute | solution.py:678
  88.2 9.3 %collective-permute-start.11 = (f32[256,128]{1,0:T(8,128)S(1)}, f32[256,128]{1,0:T(8,128)S(1)}, u32[]{:S(2)}, u32[]{:S(2)}) collective-permute-start(f32[256,128]{1,0:T(8,128)S(1)} %get-tuple-element.187), channel_id=1, source_target_pairs={{0,1},{1,0},{2,3},{3,2},{4,5},{5,4},{6,7},{7,6},{8,9},{9,8},{10,11... | collective-permute-start | bytes 393224 | tf_op jit(solution)/shard_map/ppermute | solution.py:678
  88.2 9.3 %collective-permute-start.12 = (f32[256,128]{1,0:T(8,128)S(1)}, f32[256,128]{1,0:T(8,128)S(1)}, u32[]{:S(2)}, u32[]{:S(2)}) collective-permute-start(f32[256,128]{1,0:T(8,128)S(1)} %get-tuple-element.188), channel_id=1, source_target_pairs={{0,31},{1,2},{2,1},{3,4},{4,3},{5,6},{6,5},{7,8},{8,7},{9,10},{10,... | collective-permute-start | bytes 393224 | tf_op jit(solution)/shard_map/ppermute | solution.py:678
  117.8 11.3 %collective-permute-start.15 = (f32[256,128]{1,0:T(8,128)S(1)}, f32[256,128]{1,0:T(8,128)S(1)}, u32[]{:S(2)}, u32[]{:S(2)}) collective-permute-start(f32[256,128]{1,0:T(8,128)S(1)} %get-tuple-element.211), channel_id=1, source_target_pairs={{0,24},{1,25},{2,26},{3,27},{4,28},{5,29},{6,30},{7,31},{8,16},{9,... | collective-permute-start | bytes 393224 | tf_op jit(solution)/shard_map/ppermute | solution.py:678
  120.4 8.8 %collective-permute-start.16 = (f32[256,128]{1,0:T(8,128)S(1)}, f32[256,128]{1,0:T(8,128)S(1)}, u32[]{:S(2)}, u32[]{:S(2)}) collective-permute-start(f32[256,128]{1,0:T(8,128)S(1)} %get-tuple-element.212), channel_id=1, source_target_pairs={{0,1},{1,0},{2,3},{3,2},{4,5},{5,4},{6,7},{7,6},{8,9},{9,8},{10,11... | collective-permute-start | bytes 393224 | tf_op jit(solution)/shard_map/ppermute | solution.py:678
  120.4 9.0 %collective-permute-start.17 = (f32[256,128]{1,0:T(8,128)S(1)}, f32[256,128]{1,0:T(8,128)S(1)}, u32[]{:S(2)}, u32[]{:S(2)}) collective-permute-start(f32[256,128]{1,0:T(8,128)S(1)} %get-tuple-element.213), channel_id=1, source_target_pairs={{0,31},{1,2},{2,1},{3,4},{4,3},{5,6},{6,5},{7,8},{8,7},{9,10},{10,... | collective-permute-start | bytes 393224 | tf_op jit(solution)/shard_map/ppermute | solution.py:678
  130.3 11.3 %collective-permute-start.19 = (f32[256,128]{1,0:T(8,128)S(1)}, f32[256,128]{1,0:T(8,128)S(1)}, u32[]{:S(2)}, u32[]{:S(2)}) collective-permute-start(f32[256,128]{1,0:T(8,128)S(1)} %get-tuple-element.219), channel_id=1, source_target_pairs={{0,24},{1,25},{2,26},{3,27},{4,28},{5,29},{6,30},{7,31},{8,16},{9,... | collective-permute-start | bytes 393224 | tf_op jit(solution)/shard_map/ppermute | solution.py:678
  132.8 8.8 %collective-permute-start.20 = (f32[256,128]{1,0:T(8,128)S(1)}, f32[256,128]{1,0:T(8,128)S(1)}, u32[]{:S(2)}, u32[]{:S(2)}) collective-permute-start(f32[256,128]{1,0:T(8,128)S(1)} %get-tuple-element.220), channel_id=1, source_target_pairs={{0,1},{1,0},{2,3},{3,2},{4,5},{5,4},{6,7},{7,6},{8,9},{9,8},{10,11... | collective-permute-start | bytes 393224 | tf_op jit(solution)/shard_map/ppermute | solution.py:678
  132.8 8.8 %collective-permute-start.21 = (f32[256,128]{1,0:T(8,128)S(1)}, f32[256,128]{1,0:T(8,128)S(1)}, u32[]{:S(2)}, u32[]{:S(2)}) collective-permute-start(f32[256,128]{1,0:T(8,128)S(1)} %get-tuple-element.221), channel_id=1, source_target_pairs={{0,31},{1,2},{2,1},{3,4},{4,3},{5,6},{6,5},{7,8},{8,7},{9,10},{10,... | collective-permute-start | bytes 393224 | tf_op jit(solution)/shard_map/ppermute | solution.py:678
  162.1 11.2 %collective-permute-start.24 = (f32[256,128]{1,0:T(8,128)S(1)}, f32[256,128]{1,0:T(8,128)S(1)}, u32[]{:S(2)}, u32[]{:S(2)}) collective-permute-start(f32[256,128]{1,0:T(8,128)S(1)} %get-tuple-element.245), channel_id=1, source_target_pairs={{0,24},{1,25},{2,26},{3,27},{4,28},{5,29},{6,30},{7,31},{8,16},{9,... | collective-permute-start | bytes 393224 | tf_op jit(solution)/shard_map/ppermute | solution.py:678
  164.6 8.7 %collective-permute-start.25 = (f32[256,128]{1,0:T(8,128)S(1)}, f32[256,128]{1,0:T(8,128)S(1)}, u32[]{:S(2)}, u32[]{:S(2)}) collective-permute-start(f32[256,128]{1,0:T(8,128)S(1)} %get-tuple-element.246), channel_id=1, source_target_pairs={{0,1},{1,0},{2,3},{3,2},{4,5},{5,4},{6,7},{7,6},{8,9},{9,8},{10,11... | collective-permute-start | bytes 393224 | tf_op jit(solution)/shard_map/ppermute | solution.py:678
  164.8 9.0 %collective-permute-start.26 = (f32[256,128]{1,0:T(8,128)S(1)}, f32[256,128]{1,0:T(8,128)S(1)}, u32[]{:S(2)}, u32[]{:S(2)}) collective-permute-start(f32[256,128]{1,0:T(8,128)S(1)} %get-tuple-element.247), channel_id=1, source_target_pairs={{0,31},{1,2},{2,1},{3,4},{4,3},{5,6},{6,5},{7,8},{8,7},{9,10},{10,... | collective-permute-start | bytes 393224 | tf_op jit(solution)/shard_map/ppermute | solution.py:678
  175.0 8.2 %collective-permute-start.28 = (f32[256,128]{1,0:T(8,128)S(1)}, f32[256,128]{1,0:T(8,128)S(1)}, u32[]{:S(2)}, u32[]{:S(2)}) collective-permute-start(f32[256,128]{1,0:T(8,128)S(1)} %get-tuple-element.260), channel_id=1, source_target_pairs={{0,24},{1,25},{2,26},{3,27},{4,28},{5,29},{6,30},{7,31},{8,16},{9,... | collective-permute-start | bytes 393224 | tf_op jit(solution)/shard_map/ppermute | solution.py:678
  177.4 8.8 %collective-permute-start.30 = (f32[256,128]{1,0:T(8,128)S(1)}, f32[256,128]{1,0:T(8,128)S(1)}, u32[]{:S(2)}, u32[]{:S(2)}) collective-permute-start(f32[256,128]{1,0:T(8,128)S(1)} %get-tuple-element.262), channel_id=1, source_target_pairs={{0,31},{1,2},{2,1},{3,4},{4,3},{5,6},{6,5},{7,8},{8,7},{9,10},{10,... | collective-permute-start | bytes 393224 | tf_op jit(solution)/shard_map/ppermute | solution.py:678
  (13 other events, 126.7 us)
